TPU v7x, 512 devices: a whole 4x8x8 slice. The times are simulated.
512 devices in a mesh: row: 32 (over x_hi, z, core), col: 16 (over x_lo, y).
Axes of the slice: x: 4 (x_hi: 2, x_lo: 2; x = x_hi * 2 + x_lo), y: 8, z: 8, core: 2. Of those that a mesh axis runs over, the one named last changes fastest.
Arguments:
- pair: bfloat16 [512, 512, 128], P('row', 'col'), may hold values from -6 to 6
- w_proj: bfloat16 [128, 512], replicated
- w_bias: bfloat16 [128, 4], replicated, may hold values from -0.5 to 0.5
- w_out: bfloat16 [128, 128], replicated, may hold values from -0.5 to 0.5
- token_mask: int32 [512], P('col'), may hold values from 0 to 1, as said below
Outputs:
- update: bfloat16 [512, 512, 128], P('row', 'col')
Inputs may be any that keep to these rules, and one draw needn't show every extreme that they name: `token_mask`: token 0 is real; the last 32 tokens or more are padding; real tokens before the padding have gaps.
All inputs are finite; a program needn't handle non-finite values.
Results may differ from a plain program's by a relative error of at most 0.011.
The roundings to bfloat16 on the way count: a program that leaves them out, or rounds other values in their place, can miss the bound.
Values may be sent and summed in bfloat16 or wider, within the bound.
No kernel may reach another device: no remote copies, remote signals or barrier semaphores. Data moves between devices by JAX's collectives and lax.ppermute only.
A program may use at most 128 MiB of HBM per device.

v0:
```python
import jax
import jax.numpy as jnp
from jax import lax
from jax.sharding import PartitionSpec as P


def from_root(value, axis, source):
    kept = jnp.where(lax.axis_index(axis) == source, value, 0).astype(value.dtype)
    return lax.psum(kept, axis)


def norm_rows(block):
    values = block.astype(jnp.float32)
    center = jnp.mean(values, axis=-1, keepdims=True)
    spread = jnp.mean((values - center) ** 2, axis=-1, keepdims=True)
    return ((values - center) * lax.rsqrt(spread + 1e-05)).astype(jnp.bfloat16)


def on_device(pair, w_proj, w_bias, w_out, token_mask):
    rows, cols, width = pair.shape
    heads = w_bias.shape[1]
    head_size = width // heads
    normed = norm_rows(pair)
    flat = normed.reshape(rows * cols, width)
    proj = jnp.dot(flat, w_proj, preferred_element_type=jnp.float32)
    query = (
        (proj[:, :width] * head_size ** (-0.5))
        .astype(jnp.bfloat16)
        .reshape(rows, cols, heads, head_size)
    )
    gates = proj[:, 3 * width :].astype(jnp.bfloat16).reshape(rows, cols, width)
    own_bias = jnp.dot(flat, w_bias, preferred_element_type=jnp.float32).astype(jnp.bfloat16)
    own_bias = jnp.transpose(own_bias.reshape(rows, cols, heads), (2, 0, 1))
    bias_all = lax.all_gather(own_bias, "col", axis=2, tiled=True)
    ratio = lax.axis_size("row") // lax.axis_size("col")
    base = lax.axis_index("col") * ratio
    parts_list = []
    for member in range(ratio):
        parts_list.append(from_root(bias_all, "row", base + member))
    bias = jnp.concatenate(parts_list, axis=1)
    mask_row = token_mask.astype(jnp.bfloat16).reshape(1, cols)

    def block_step(carry, inputs):
        keys, values, mask_block, offset = inputs
        largest, total, accum = carry
        scores = jnp.einsum("rjhd,rkhd->hrjk", query, keys, preferred_element_type=jnp.float32)
        bias_block = lax.dynamic_slice_in_dim(bias, offset, cols, 2).astype(jnp.float32)
        masked = (mask_block.astype(jnp.float32) - 1.0) * 1000000000.0
        scores = scores + bias_block[:, None, :, :] + masked[None, None, None, :]
        newest = jnp.maximum(largest, jnp.max(scores, axis=-1))
        scale_old = jnp.exp(largest - newest)
        expo = jnp.exp(scores - newest[..., None])
        total = total * scale_old + jnp.sum(expo, axis=-1)
        added = jnp.einsum(
            "hrjk,rkhd->rjhd", expo.astype(jnp.bfloat16), values, preferred_element_type=jnp.float32
        )
        accum = accum * jnp.transpose(scale_old, (1, 2, 0))[..., None] + added
        carry = (newest, total, accum)
        return (carry, None)

    init = (
        jnp.full((heads, rows, cols), -1e30, jnp.float32),
        jnp.zeros((heads, rows, cols), jnp.float32),
        jnp.zeros((rows, cols, heads, head_size), jnp.float32),
    )
    pairs_kv = proj[:, width : 3 * width].astype(jnp.bfloat16).reshape(rows, cols, 2 * width)
    block = lax.all_gather(pairs_kv, "col", axis=1, tiled=True)
    mask_piece = lax.all_gather(mask_row, "col", axis=1, tiled=True)
    keys = block[:, :, :width].reshape(rows, block.shape[1], heads, head_size)
    values = block[:, :, width:].reshape(rows, block.shape[1], heads, head_size)
    carry = init
    run_keys = keys
    run_values = values
    count = run_keys.shape[1] // cols
    run_keys = jnp.transpose(run_keys.reshape(rows, count, cols, heads, head_size), (1, 0, 2, 3, 4))
    run_values = jnp.transpose(
        run_values.reshape(rows, count, cols, heads, head_size), (1, 0, 2, 3, 4)
    )
    mask_blocks = mask_piece.reshape(count, cols)
    offsets = jnp.arange(count, dtype=jnp.int32) * cols
    carry, unused = lax.scan(block_step, carry, (run_keys, run_values, mask_blocks, offsets))
    largest, total, accum = carry
    attended = accum / jnp.transpose(total, (1, 2, 0))[..., None]
    gated = (
        attended.reshape(rows, cols, width) * jax.nn.sigmoid(gates.astype(jnp.float32))
    ).astype(jnp.bfloat16)
    result = jnp.dot(gated.reshape(rows * cols, width), w_out, preferred_element_type=jnp.float32)
    return result.astype(jnp.bfloat16).reshape(rows, cols, width)


def solution(mesh):
    in_specs = (P("row", "col", None), P(), P(), P(), P("col"))
    out_specs = P("row", "col", None)
    return jax.shard_map(
        on_device, mesh=mesh, in_specs=in_specs, out_specs=out_specs, check_vma=False
    )
```

profile of v0, /device:TPU:1, one launch (start us, length us, event | category | flops | bytes accessed | tf_op | source)
XLA Modules:
  0.0 493.4 jit_solution(3689532168035376962)
XLA Ops:
  11.8 30.3 %all_gather.10 = bf16[4,16,512]{1,0,2:T(4,128)(2,1)S(1)} all-gather(bf16[4,16,32]{1,0,2:T(4,128)(2,1)S(1)} %bitcast.63), channel_id=1, replica_groups=mesh['row'=32,'col'=16] {'col'}, dimensions={2}, use_global_device_ids=true | all-gather | bytes 69632 | tf_op jit(solution)/shard_map/all_gather | solution.py:34
  47.4 24.4 %all-reduce = bf16[512]{0:T(512)(128)(2,1)S(1)} all-reduce(bf16[512]{0:T(512)(128)(2,1)S(1)} %dynamic-update-slice), channel_id=2, replica_groups=mesh['row'=32,'col'=16] {'col'}, use_global_device_ids=true, to_apply=%add | all-reduce | flops 512 | bytes 2048
  71.9 253.3 %all-reduce.4.cloned.1.call-done = (bf16[4,16,512]{1,0,2:T(4,128)(2,1)}, bf16[4,16,512]{1,0,2:T(4,128)(2,1)}) async-done(((bf16[4,16,512]{1,0,2:T(4,128)(2,1)}, bf16[4,16,512]{1,0,2:T(4,128)(2,1)}), (bf16[4,16,512]{1,0,2:T(4,128)(2,1)}, bf16[4,16,512]{1,0,2:T(4,128)(2,1)})) %all-reduce.4.cloned.1.call-update) | async-done | bytes 131088 | tf_op jit(solution)/shard_map/psum | solution.py:9
  327.8 4.9 fusion.25
  332.6 4.3 copy.35
  337.0 10.3 %reshape_reshape.6 = bf16[16,16,32,4,32]{2,1,4,3,0:T(8,128)(2,1)} reshape(bf16[16,512,128]{1,2,0:T(8,128)(2,1)} %copy.35) | data formatting | bytes 4194304 | tf_op jit(solution)/shard_map/reshape;reshape | solution.py:75
  347.3 12.8 %copy.40 = bf16[16,16,32,4,32]{4,2,1,3,0:T(8,128)(2,1)} copy(bf16[16,16,32,4,32]{2,0,4,3,1:T(8,128)(2,1)} %bitcast.57) | data formatting | bytes 4194304
  360.1 4.5 copy.39
  364.5 10.2 %reshape_reshape.7 = bf16[16,16,32,4,32]{2,1,4,3,0:T(8,128)(2,1)} reshape(bf16[16,512,128]{1,2,0:T(8,128)(2,1)} %copy.39) | data formatting | bytes 4194304 | tf_op jit(solution)/shard_map/reshape;reshape | solution.py:77
  374.7 8.8 %copy.43 = bf16[16,16,32,4,32]{2,4,3,1,0:T(8,128)(2,1)} copy(bf16[16,16,32,4,32]{2,0,4,3,1:T(8,128)(2,1)} %bitcast.58) | data formatting | bytes 4194304
  383.6 100.4 %while.17 = (s32[]{:T(128)}, f32[4,16,32]{2,1,0:T(8,128)S(1)}, f32[4,16,32]{2,1,0:T(8,128)S(1)}, f32[16,32,4,32]{1,3,2,0:T(8,128)S(1)}, bf16[16,16,32,4,32]{4,2,...) while((s32[]{:T(128)}, f32[4,16,32]{2,1,0:T(8,128)S(1)}, ...), condition=%wide.region_7.8_spmd.clone, body=%wide.region_4.7_spmd.clone.sunk | while | flops 8994918 | bytes 2704895 | solution.py:81
  386.6 1.5 fusion.46
  392.8 1.5 fusion.46
  399.1 1.5 fusion.46
  400.9 1.4 fusion.50
  405.4 1.5 fusion.46
  411.7 1.5 fusion.46
  413.5 1.4 fusion.50
  417.9 1.5 fusion.46
  424.2 1.5 fusion.46
  426.0 1.4 fusion.50
  430.5 1.5 fusion.46
  436.8 1.5 fusion.46
  438.6 1.4 fusion.50
  443.0 1.5 fusion.46
  449.3 1.5 fusion.46
  451.1 1.4 fusion.50
  455.6 1.5 fusion.46
  461.9 1.5 fusion.46
  468.2 1.5 fusion.46
  474.4 1.5 fusion.46
  480.7 1.5 fusion.46
  (214 shorter events, 49.0 us)
Async XLA Ops:
  7.4 36.2 %copy-start = (bf16[128,512]{1,0:T(8,128)(2,1)S(1)}, bf16[128,512]{1,0:T(8,128)(2,1)}, u32[]{:S(2)}) copy-start(bf16[128,512]{1,0:T(8,128)(2,1)} %param.8) | copy-start | bytes 393220
  7.4 37.8 %copy-start.2 = (s32[32]{0:T(128)S(1)}, s32[32]{0:T(128)}, u32[]{:S(2)}) copy-start(s32[32]{0:T(128)} %param.11) | copy-start | bytes 388
  7.4 317.8 %all-reduce.4.cloned.1.call-start = ((), (), s32[]{:S(2)}) async-start(), calls=%async_computation.1 | async-start | bytes 2097152 | tf_op jit(solution)/shard_map/psum | solution.py:9
  43.5 284.2 %all-gather.3.cloned.1.call-start = ((), (), s32[]{:S(2)}) async-start(), calls=%async_computation | async-start | bytes 4456448 | tf_op jit(solution)/shard_map/all_gather | solution.py:67
  383.6 101.5 %copy-start.1 = (bf16[128,128]{1,0:T(8,128)(2,1)S(1)}, bf16[128,128]{1,0:T(8,128)(2,1)}, u32[]{:S(2)}) copy-start(bf16[128,128]{1,0:T(8,128)(2,1)} %param.10) | copy-start | bytes 98308
Sparse Core Ops, SparseCore 0:
  43.6 281.4 all-reduce.3
Sparse Core Ops, SparseCore 1:
  46.1 76.9 all-gather.2
where the time goes:
time: 497 us; the launch traced here: 493 us
  waiting for transfers between devices  253 us (51%)
  local copies, waits for them, and re-layouts  76.2 us (15%)
  blocking collectives  54.7 us (11%)
  matrix products  48.2 us (10%)
  loops' own time  34.5 us (7%)
  between operations  15.7 us (3%)
  other arithmetic  10.8 us (2%)
    psum x1, waiting for transfers between devices, from_root(): return lax.psum(kept, axis)  253 us
    another operation x1, loops' own time, on_device(): lax.scan(block_step, carry, (run_keys, run_values, mask_blocks, offsets))  34.5 us
    all_gather x1, blocking collectives, on_device(): bias_all = lax.all_gather(own_bias, 'col', axis=2, tiled=True)  30.3 us
    unnamed x1, blocking collectives  24.4 us
    dot_general x16, matrix products, block_step(): jnp.einsum('rjhd,rkhd->hrjk', query, keys, preferred_element_type=jnp.flo...  23.3 us
    unnamed x12, local copies, waits for them, and re-layouts  23.2 us
    dot_general x16, matrix products, block_step(): jnp.einsum('hrjk,rkhd->rjhd', expo.astype(jnp.bfloat16), values, preferre...  23 us
    dynamic_slice x16, local copies, waits for them, and re-layouts, on_device(): lax.scan(block_step, carry, (run_keys, run_values, mask_blocks, offsets))  10.6 us
  transfers between devices with their start and end apart: 2, of which 1 were waited for; matrix products, arithmetic and copies ran while one was open for 1% of the time, Pallas kernels for 0%

commit v1 on v0

v1 whole, which is shorter than its diff:
```python
import functools

import jax
import jax.numpy as jnp
from jax import lax
from jax.experimental import pallas as pl
from jax.experimental.pallas import tpu as pltpu
from jax.sharding import PartitionSpec as P

F32 = jnp.float32
BF16 = jnp.bfloat16
VMEM = pl.BlockSpec(memory_space=pltpu.VMEM)
SMEM = pl.BlockSpec(memory_space=pltpu.SMEM)

SPLIT = 4
MASK_ROWS = 16


def norm_rows(values):
    center = jnp.mean(values, axis=-1, keepdims=True)
    shifted = values - center
    spread = jnp.mean(shifted * shifted, axis=-1, keepdims=True)
    return (shifted * lax.rsqrt(spread + 1e-05)).astype(BF16)


def pre_kernel(rows, cols, heads, pair_ref, w_bias_ref, normed_ref, spread_ref):
    normed = norm_rows(pair_ref[...].astype(F32))
    normed_ref[...] = normed
    width = normed.shape[1]
    lane = lax.broadcasted_iota(jnp.int32, (width, width), 1) // cols
    w_bias = w_bias_ref[...].astype(F32)
    wide = jnp.zeros((width, width), F32)
    for head in range(heads):
        wide = jnp.where(lane == head, w_bias[:, head : head + 1], wide)
    product = jnp.dot(normed, wide.astype(BF16), preferred_element_type=F32)
    column = lax.broadcasted_iota(jnp.int32, product.shape, 0) % cols
    place = lax.broadcasted_iota(jnp.int32, product.shape, 1) % cols
    product = jnp.where(column == place, product, 0.0)
    bias = jnp.sum(product.reshape(rows, cols, width), axis=1).astype(BF16)
    for member in range(spread_ref.shape[0]):
        spread_ref[member] = bias


def pack_kernel(normed_ref, bias_ref, mask_ref, send_ref):
    members = send_ref.shape[0]
    width = normed_ref.shape[1]
    part = normed_ref.shape[0] // SPLIT
    blocks = bias_ref.shape[0] // SPLIT
    depth = blocks * bias_ref.shape[1]
    for member in range(members):
        query_block, sub = divmod(member, SPLIT)
        send_ref[member, 0:part] = normed_ref[sub * part : (sub + 1) * part]
        chosen = bias_ref[query_block * blocks : (query_block + 1) * blocks]
        send_ref[member, part : part + depth] = chosen.reshape(depth, width)
        send_ref[member, part + depth :] = mask_ref[...]


def attend_kernel(
    heads, ids_ref, block_ref, other_ref, w_proj_ref, w_out_ref, out_ref, bias_ref, scores_ref
):
    members, _, width = block_ref.shape
    own_rows, cols = out_ref.shape[1], out_ref.shape[2]
    part = own_rows * cols
    depth = other_ref.shape[1]
    keys_count = members * cols
    queries = SPLIT * cols
    head_size = width // heads
    lanes = members * width
    first = ids_ref[0]
    parity = ids_ref[1]

    for member in range(members):
        mask = block_ref[member, part + depth :].astype(F32)[0:1]
        masked = (mask - 1.0) * 1e9
        own = block_ref[member, part : part + depth].astype(F32) + masked
        other = other_ref[member].astype(F32) + masked
        bias_ref[member, :, parity] = own.reshape(SPLIT, depth // SPLIT, width)
        bias_ref[member, :, 1 - parity] = other.reshape(SPLIT, depth // SPLIT, width)

    shape = (heads, cols, width)
    head_of_row = lax.broadcasted_iota(jnp.int32, shape, 0)
    head_of_lane = lax.broadcasted_iota(jnp.int32, shape, 2) // head_size
    same = (head_of_row == head_of_lane).astype(F32).astype(BF16)
    ones = jnp.broadcast_to(same[None], (members,) + shape).reshape(lanes, width)
    lane_head = lax.broadcasted_iota(jnp.int32, (queries, width), 1) // cols

    def spread(values):
        wide = values.reshape(members, 1, cols, width) * same[None]
        return wide.reshape(lanes, width)

    for row in range(own_rows):
        entries = block_ref[:, row * cols : (row + 1) * cols].reshape(keys_count, width)
        asking = block_ref[pl.ds(first, SPLIT), row * cols : (row + 1) * cols]
        asking = asking.reshape(queries, width)
        query = jnp.dot(asking, w_proj_ref[:, :width], preferred_element_type=F32)
        query = (query * head_size ** (-0.5)).astype(BF16)
        gates = jnp.dot(asking, w_proj_ref[:, 3 * width :], preferred_element_type=F32)
        gates = gates.astype(BF16).astype(F32)
        both = jnp.dot(entries, w_proj_ref[:, width : 3 * width], preferred_element_type=F32)
        both = both.astype(BF16)
        keys = spread(both[:, :width])
        values = jnp.concatenate([spread(both[:, width:]), ones], axis=1)

        scores = lax.dot_general(
            query, keys, (((1,), (1,)), ((), ())), preferred_element_type=F32
        )
        largest = None
        for member in range(members):
            piece = scores[:, member * width : (member + 1) * width]
            piece = piece + bias_ref[member].reshape(queries, width)
            scores_ref[row % 2, :, member * width : (member + 1) * width] = piece
            largest = piece if largest is None else jnp.maximum(largest, piece)
        top = jnp.zeros((queries, width), F32)
        for head in range(heads):
            chosen = jnp.where(lane_head == head, largest, -jnp.inf)
            top = jnp.where(lane_head == head, jnp.max(chosen, axis=-1, keepdims=True), top)
        pieces = []
        for member in range(members):
            piece = scores_ref[row % 2, :, member * width : (member + 1) * width]
            pieces.append(jnp.exp(piece - top).astype(BF16))
        weights = jnp.concatenate(pieces, axis=1)
        sums = jnp.dot(weights, values, preferred_element_type=F32)
        attended = sums[:, :width] / sums[:, width:]
        gated = (attended * jax.nn.sigmoid(gates)).astype(BF16)
        result = jnp.dot(gated, w_out_ref[...], preferred_element_type=F32).astype(BF16)
        out_ref[:, row] = result.reshape(SPLIT, cols, width)


def on_device(pair, w_proj, w_bias, w_out, token_mask, *, row_size, col_size):
    rows, cols, width = pair.shape
    heads = w_bias.shape[1]
    own_rows = rows // SPLIT
    half = row_size // 2
    queries = SPLIT * cols
    depth = queries // 2
    part = own_rows * cols
    chunk = part + depth + MASK_ROWS

    normed, spread = pl.pallas_call(
        functools.partial(pre_kernel, rows, cols, heads),
        out_shape=(
            jax.ShapeDtypeStruct((rows * cols, width), BF16),
            jax.ShapeDtypeStruct((half, rows, width), BF16),
        ),
        in_specs=[VMEM, VMEM],
        out_specs=(VMEM, VMEM),
    )(pair.reshape(rows * cols, width), w_bias)

    same_core = [[2 * n + core for n in range(half)] for core in range(2)]
    bias = lax.all_to_all(spread, "row", 0, 0, axis_index_groups=same_core, tiled=True)

    mask = jnp.tile(token_mask, width // cols).astype(BF16)
    mask = jnp.broadcast_to(mask[None], (MASK_ROWS, width))
    send = pl.pallas_call(
        pack_kernel,
        out_shape=jax.ShapeDtypeStruct((col_size, chunk, width), BF16),
        in_specs=[VMEM, VMEM, VMEM],
        out_specs=VMEM,
    )(normed, bias, mask)
    block = lax.all_to_all(send, "col", 0, 0, tiled=True)

    swap = [(r, r ^ 1) for r in range(row_size)]
    other = lax.ppermute(block[:, part : part + depth], "row", swap)

    ids = jnp.stack([lax.axis_index("col") // SPLIT * SPLIT, lax.axis_index("row") % 2])
    answer = pl.pallas_call(
        functools.partial(attend_kernel, heads),
        out_shape=jax.ShapeDtypeStruct((SPLIT, own_rows, cols, width), BF16),
        in_specs=[SMEM, VMEM, VMEM, VMEM, VMEM],
        out_specs=VMEM,
        scratch_shapes=[
            pltpu.VMEM((col_size, SPLIT, 2, depth // SPLIT, width), F32),
            pltpu.VMEM((2, queries, col_size * width), F32),
        ],
        compiler_params=pltpu.CompilerParams(vmem_limit_bytes=40 * 1024 * 1024),
    )(ids.astype(jnp.int32), block, other, w_proj, w_out)

    near = [[SPLIT * g + m for m in range(SPLIT)] for g in range(col_size // SPLIT)]
    back = lax.all_to_all(answer, "col", 0, 0, axis_index_groups=near, tiled=True)
    return back.reshape(rows, cols, width)


def solution(mesh):
    in_specs = (P("row", "col", None), P(), P(), P(), P("col"))
    out_specs = P("row", "col", None)
    body = functools.partial(on_device, row_size=mesh.shape["row"], col_size=mesh.shape["col"])
    return jax.shard_map(body, mesh=mesh, in_specs=in_specs, out_specs=out_specs, check_vma=False)
```

time: 497 us -> 76.4 us (0.15)
  waiting for transfers between devices: 253 us -> 9.79 us
  local copies, waits for them, and re-layouts: 76.2 us -> 2.8 us
  matrix products: 48.2 us -> 0 us
  loops' own time: 34.5 us -> 0 us
  blocking collectives: 54.7 us -> 34.6 us
  starting transfers between devices: 0.05 us -> 19.5 us
  between operations: 15.7 us -> 0.09 us
  other arithmetic: 10.8 us -> 0.08 us
  Pallas kernels: 0 us -> 8.67 us
    psum x1 -> x0, waiting for transfers between devices: 253 us -> none  [from_root(): return lax.psum(kept, axis)]
    dot_general x35 -> x0, matrix products: 48.2 us -> none  [the longest x16 23.3 us: block_step(): jnp.einsum('rjhd,rkhd->hrjk', query, keys, preferred_element_type=jnp.flo...]
    all_to_all x0 -> x2, blocking collectives: none -> 34.6 us  [the longest x1 26.5 us: on_device(): block = lax.all_to_all(send, 'col', 0, 0, tiled=True)]
    another operation x1 -> x0, loops' own time: 34.5 us -> none  [on_device(): lax.scan(block_step, carry, (run_keys, run_values, mask_blocks, offsets))]
    all_gather x1 -> x0, blocking collectives: 30.3 us -> none  [on_device(): bias_all = lax.all_gather(own_bias, 'col', axis=2, tiled=True)]
    unnamed x1 -> x0, blocking collectives: 24.4 us -> none
    unnamed x12 -> x10, local copies, waits for them, and re-layouts: 23.2 us -> 2.08 us
    another operation x2 -> x1, local copies, waits for them, and re-layouts: 20.5 us -> 0.01 us  [on_device(): mask = jnp.tile(token_mask, width // cols).astype(BF16)]
  transfers between devices with their start and end apart: 2 -> 2, of which waited for: 1 -> 2; matrix products, arithmetic and copies ran while one was open for 1% -> 0% of each run, Pallas kernels for 0% -> 0%
where the time goes in v1:
time: 76.4 us; the launch traced here: 75.5 us
  blocking collectives  34.6 us (45%)
  starting transfers between devices  19.5 us (26%)
  waiting for transfers between devices  9.79 us (13%)
  Pallas kernels  8.67 us (11%)
  local copies, waits for them, and re-layouts  2.8 us (4%)
    all_to_all x1, blocking collectives, on_device(): block = lax.all_to_all(send, 'col', 0, 0, tiled=True)  26.5 us
    all_to_all x1, starting transfers between devices, on_device(): lax.all_to_all(spread, 'row', 0, 0, axis_index_groups=same_core, tiled=True)  13.6 us
    all_to_all x1, waiting for transfers between devices, on_device(): lax.all_to_all(spread, 'row', 0, 0, axis_index_groups=same_core, tiled=True)  8.76 us
    all_to_all x1, blocking collectives, on_device(): lax.all_to_all(answer, 'col', 0, 0, axis_index_groups=near, tiled=True)  8.14 us
    ppermute x1, starting transfers between devices, on_device(): other = lax.ppermute(block[:, part:part + depth], 'row', swap)  5.91 us
    pallas_call x1, Pallas kernels, on_device(): pl.pallas_call(functools.partial(attend_kernel, heads), out_shape=jax.Sha...  4.63 us
    pallas_call x1, Pallas kernels, on_device(): pl.pallas_call(functools.partial(pre_kernel, rows, cols, heads), out_shap...  2.09 us
    unnamed x10, local copies, waits for them, and re-layouts  2.08 us
  transfers between devices with their start and end apart: 2, of which 2 were waited for; matrix products, arithmetic and copies ran while one was open for 0% of the time, Pallas kernels for 0%

profile of v1, /device:TPU:1, one launch (start us, length us, event | category | flops | bytes accessed | tf_op | source)
XLA Modules:
  0.0 75.5 jit_solution(3316500238754223008)
XLA Ops:
  0.0 1.4 %copy.6.w_bias_ref = bf16[128,4]{1,0:T(8,128)(2,1)} copy(bf16[128,4]{0,1:T(4,128)(2,1)} %param.7) | data formatting | bytes 2048 | tf_op args[2]
  1.4 2.1 %shard_map.55 = (bf16[512,128]{1,0:T(8,128)(2,1)}, bf16[16,16,128]{2,1,0:T(8,128)(2,1)}) custom-call(bf16[512,128]{1,0:T(8,128)(2,1)} %bitcast.5, bf16[128,4]{1,0:T(8,128)(2,1)} %copy.6.w_bias_ref), custom_call_target="tpu_custom_call" | custom-call | tf_op jit(solution)/shard_map/pallas_call | solution.py:139
  3.5 0.0 copy-start.3
  3.5 13.6 %all-to-all-start = ((bf16[16,16,128]{2,1,0:T(8,128)(2,1)}), bf16[16,16,128]{2,1,0:T(8,128)(2,1)S(1)}, u32[]{:S(2)}, u32[]{:S(2)}) async-start(bf16[16,16,128]{2,1,0:T(8,128)(2,1)} %get-tuple-element.8), calls=%async_computation | async-start | bytes 131072 | tf_op jit(solution)/shard_map/all_to_all | solution.py:150
  17.0 0.0 copy-done.3
  17.1 0.1 convert_element_type.12
  17.2 8.8 %all-to-all-done.bias_ref = bf16[16,16,128]{2,1,0:T(8,128)(2,1)S(1)} async-done(((bf16[16,16,128]{2,1,0:T(8,128)(2,1)}), bf16[16,16,128]{2,1,0:T(8,128)(2,1)S(1)}, u32[]{:S(2)}, u32[]{:S(2)}) %all-to-all-start) | async-done | bytes 65568 | tf_op jit(solution)/shard_map/all_to_all | solution.py:150
  25.9 0.0 copy-start.2
  25.9 0.6 broadcast_in_dim.2.mask_ref
  26.5 0.0 copy-done.2
  26.6 2.0 %shard_map.56 = bf16[16,208,128]{2,1,0:T(8,128)(2,1)} custom-call(bf16[512,128]{1,0:T(8,128)(2,1)} %get-tuple-element.7.normed_ref, bf16[16,16,128]{2,1,0:T(8,128)(2,1)} %copy-done.2, bf16[16,128]{1,0:T(8,128)(2,1)} %broadcast_in_dim.2.mask_ref), custom_call_target="tpu_custom_call" | custom-call | tf_op jit(solution)/shard_map/pallas_call | solution.py:154
  28.5 26.5 %all_to_all.15.block_ref = bf16[16,208,128]{2,1,0:T(8,128)(2,1)S(1)} all-to-all(bf16[16,208,128]{2,1,0:T(8,128)(2,1)} %shard_map.56), channel_id=1, replica_groups=mesh['row'=32,'col'=16] {'col'}, dimensions={0} | all-to-all | bytes 1703936 | tf_op jit(solution)/shard_map/all_to_all | solution.py:160
  55.0 0.0 copy-start
  55.0 5.9 %collective-permute-start = (bf16[16,64,128]{2,1,0:T(8,128)(2,1)S(1)}, bf16[16,64,128]{2,1,0:T(8,128)(2,1)S(1)}, u32[]{:S(2)}, u32[]{:S(2)}) collective-permute-start(bf16[16,64,128]{2,1,0:T(8,128)(2,1)S(1)} %slice.4), channel_id=1, source_target_pairs={{0,16},{16,0},{32,48},{48,32},{64,80},{80,64},{96,112},{112,96},{1... | collective-permute-start | bytes 786440 | tf_op jit(solution)/shard_map/ppermute | solution.py:163
  61.0 0.0 copy-start.1
  61.0 0.1 pad_add_fusion.ids_ref
  61.1 1.0 %collective-permute-done.other_ref = bf16[16,64,128]{2,1,0:T(8,128)(2,1)S(1)} collective-permute-done((bf16[16,64,128]{2,1,0:T(8,128)(2,1)S(1)}, bf16[16,64,128]{2,1,0:T(8,128)(2,1)S(1)}, u32[]{:S(2)}, u32[]{:S(2)}) %collective-permute-start) | collective-permute-done | bytes 262176 | tf_op jit(solution)/shard_map/ppermute | solution.py:163
  62.1 0.0 copy-done
  62.1 0.0 copy-done.1
  62.1 4.6 %shard_map.57 = bf16[4,4,32,128]{3,2,1,0:T(8,128)(2,1)S(1)} custom-call(s32[2]{0:T(128)S(1)} %pad_add_fusion.ids_ref, bf16[16,208,128]{2,1,0:T(8,128)(2,1)S(1)} %all_to_all.15.block_ref, bf16[16,64,128]{2,1,0:T(8,128)(2,1)S(1)} %collective-permute-done.other_ref, bf16[128,512]{1,0:T(8,128)(2,1)S(1)} %copy-done, bf16[128,128]{1,0:T(8,128)(2,1)S(1)} %copy-done.1), custom_call_target="tpu_custom_call" | custom-call | tf_op jit(solution)/shard_map/pallas_call | solution.py:166
  66.7 8.1 %all_to_all.16 = bf16[4,4,32,128]{3,2,1,0:T(8,128)(2,1)S(1)} all-to-all(bf16[4,4,32,128]{3,2,1,0:T(8,128)(2,1)S(1)} %shard_map.57), channel_id=1, replica_groups={{0,1,2,3},{4,5,6,7},{8,9,10,11},{12,13,14,15},{16,17,18,19},{20,21,22,2..., dimensions={0} | all-to-all | bytes 262144 | tf_op jit(solution)/shard_map/all_to_all | solution.py:179
  74.9 0.7 copy.8
  (3 shorter events, 0.0 us)
Async XLA Ops:
  3.5 13.6 %copy-start.3 = (s32[32]{0:T(128)S(1)}, s32[32]{0:T(128)}, u32[]{:S(2)}) copy-start(s32[32]{0:T(128)} %param.9) | copy-start | bytes 388
  3.5 22.4 %all-to-all-start = ((bf16[16,16,128]{2,1,0:T(8,128)(2,1)}), bf16[16,16,128]{2,1,0:T(8,128)(2,1)S(1)}, u32[]{:S(2)}, u32[]{:S(2)}) async-start(bf16[16,16,128]{2,1,0:T(8,128)(2,1)} %get-tuple-element.8), calls=%async_computation | async-start | bytes 131072 | tf_op jit(solution)/shard_map/all_to_all | solution.py:150
  25.9 0.6 copy-start.2
  55.0 7.1 %copy-start = (bf16[128,512]{1,0:T(8,128)(2,1)S(1)}, bf16[128,512]{1,0:T(8,128)(2,1)}, u32[]{:S(2)}) copy-start(bf16[128,512]{1,0:T(8,128)(2,1)} %w_proj_ref.1) | copy-start | bytes 393220
  55.0 7.1 %collective-permute-start = (bf16[16,64,128]{2,1,0:T(8,128)(2,1)S(1)}, bf16[16,64,128]{2,1,0:T(8,128)(2,1)S(1)}, u32[]{:S(2)}, u32[]{:S(2)}) collective-permute-start(bf16[16,64,128]{2,1,0:T(8,128)(2,1)S(1)} %slice.4), channel_id=1, source_target_pairs={{0,16},{16,0},{32,48},{48,32},{64,80},{80,64},{96,112},{112,96},{1... | collective-permute-start | bytes 786440 | tf_op jit(solution)/shard_map/ppermute | solution.py:163
  61.0 1.1 %copy-start.1 = (bf16[128,128]{1,0:T(8,128)(2,1)S(1)}, bf16[128,128]{1,0:T(8,128)(2,1)}, u32[]{:S(2)}) copy-start(bf16[128,128]{1,0:T(8,128)(2,1)} %w_out_ref.1) | copy-start | bytes 98308

commit v2 on v1

v2 whole, which is shorter than its diff:
```python
import functools

import jax
import jax.numpy as jnp
from jax import lax
from jax.experimental import pallas as pl
from jax.experimental.pallas import tpu as pltpu
from jax.sharding import PartitionSpec as P

F32 = jnp.float32
BF16 = jnp.bfloat16
VMEM = pl.BlockSpec(memory_space=pltpu.VMEM)
ANY = pl.BlockSpec(memory_space=pl.ANY)

SPLIT = 4
CORES = 2


def norm_rows(values):
    center = jnp.mean(values, axis=-1, keepdims=True)
    shifted = values - center
    spread = jnp.mean(shifted * shifted, axis=-1, keepdims=True)
    return (shifted * lax.rsqrt(spread + 1e-05)).astype(BF16)


def norm_kernel(rows, cols, pair_ref, w_bias_ref, mask_ref, send_ref, spread_ref):
    normed = norm_rows(pair_ref[...].astype(F32))
    width = normed.shape[1]
    part = normed.shape[0] // SPLIT
    for member in range(send_ref.shape[0]):
        sub = member % SPLIT
        send_ref[member, 0:part] = normed[sub * part : (sub + 1) * part]

    heads = w_bias_ref.shape[0]
    head_of_row = lax.broadcasted_iota(jnp.int32, (width, width), 0) // cols
    w_bias = w_bias_ref[...].astype(F32)
    wide = jnp.zeros((width, width), F32)
    for head in range(heads):
        wide = jnp.where(head_of_row == head, w_bias[head : head + 1], wide)
    product = lax.dot_general(
        normed, wide.astype(BF16), (((1,), (1,)), ((), ())), preferred_element_type=F32
    )
    column = lax.broadcasted_iota(jnp.int32, product.shape, 0) % cols
    place = lax.broadcasted_iota(jnp.int32, product.shape, 1) % cols
    product = jnp.where(column == place, product, 0.0)
    bias = jnp.sum(product.reshape(rows, cols, width), axis=1).astype(BF16)
    masked = (mask_ref[...].astype(F32) - 1.0) * 1e9
    masked = jnp.concatenate([masked] * heads, axis=1)
    bias = (bias.astype(F32) + masked).astype(BF16)
    for member in range(spread_ref.shape[0]):
        spread_ref[member] = bias


def pack_kernel(bias_ref, half_ref, send_ref, done):
    del half_ref
    members, chunk, _ = send_ref.shape
    depth = bias_ref.shape[1]
    copies = [
        pltpu.make_async_copy(
            bias_ref.at[member // SPLIT],
            send_ref.at[member, pl.ds(chunk - depth, depth)],
            done.at[member],
        )
        for member in range(members)
    ]
    for copy in copies:
        copy.start()
    for copy in copies:
        copy.wait()


def project_kernel(heads, cols, own_rows, block_ref, w_proj_ref, w_out_ref, made_ref):
    members, _, width = block_ref.shape
    head_size = width // heads
    keys_count = members * cols
    queries = SPLIT * cols
    first = lax.axis_index("col") // SPLIT * SPLIT
    for row in range(own_rows):
        entries = block_ref[:, row * cols : (row + 1) * cols].reshape(keys_count, width)
        made_ref[row, :keys_count] = jnp.dot(
            entries, w_proj_ref[:, width : 3 * width], preferred_element_type=F32
        ).astype(BF16)
        asking = block_ref[pl.ds(first, SPLIT), row * cols : (row + 1) * cols]
        asking = asking.reshape(queries, width)
        query = jnp.dot(asking, w_proj_ref[:, :width], preferred_element_type=F32)
        made_ref[row, keys_count:, :width] = (query * head_size ** (-0.5)).astype(BF16)
        gates = jnp.dot(asking, w_proj_ref[:, 3 * width :], preferred_element_type=F32)
        made_ref[row, keys_count:, width:] = gates.astype(BF16)
    made_ref[own_rows, :width, :width] = w_out_ref[...]


def attend_kernel(heads, cols, block_ref, other_ref, made_ref, out_ref, bias_ref):
    members, depth, width = other_ref.shape
    own_rows = made_ref.shape[0] - 1
    queries = SPLIT * cols
    keys_count = members * cols
    group = width // cols
    part = block_ref.shape[1] - depth
    parity = lax.axis_index("row") % CORES

    segment = lax.broadcasted_iota(jnp.int32, (1, width), 1) // cols
    for turn in range(members // group):
        for source in range(CORES):
            turned = []
            for piece in range(group):
                member = turn * group + piece
                value = other_ref[member] if source else block_ref[member, part:]
                value = value.astype(F32)
                turned.append([value] + [pltpu.roll(value, cols * d, 1) for d in range(1, group)])
            core = 1 - parity if source else parity
            for head in range(heads):
                value = turned[0][-head % group]
                for piece in range(1, group):
                    value = jnp.where(segment == piece, turned[piece][(piece - head) % group], value)
                value = value.reshape(SPLIT, depth // SPLIT, width)
                bias_ref[head, :, core, :, turn * width : (turn + 1) * width] = value

    lane_head = lax.broadcasted_iota(jnp.int32, (1, width), 1) // (width // heads)
    w_out = made_ref[own_rows, :width, :width]
    ones = jnp.ones((keys_count, width), BF16)
    for row in range(own_rows):
        query = made_ref[row, keys_count:, :width].astype(F32)
        values = jnp.concatenate([made_ref[row, :keys_count, width:], ones], axis=1)
        above = jnp.zeros((queries, width), F32)
        below = jnp.zeros((queries, width), F32)
        for head in range(heads):
            chosen = jnp.where(lane_head == head, query, 0.0).astype(BF16)
            scores = lax.dot_general(
                chosen,
                made_ref[row, :keys_count, :width],
                (((1,), (1,)), ((), ())),
                preferred_element_type=F32,
            )
            scores = scores + bias_ref[head].reshape(queries, keys_count)
            top = jnp.max(scores, axis=-1, keepdims=True)
            weights = jnp.exp(scores - top).astype(BF16)
            sums = jnp.dot(weights, values, preferred_element_type=F32)
            above = jnp.where(lane_head == head, sums[:, :width], above)
            below = jnp.where(lane_head == head, sums[:, width:], below)
        gates = made_ref[row, keys_count:, width:].astype(F32)
        gated = (above / below * jax.nn.sigmoid(gates)).astype(BF16)
        result = jnp.dot(gated, w_out, preferred_element_type=F32).astype(BF16)
        out_ref[:, row] = result.reshape(SPLIT, cols, width)


def on_device(pair, w_proj, w_bias, w_out, token_mask, *, row_size, col_size):
    rows, cols, width = pair.shape
    heads = w_bias.shape[1]
    own_rows = rows // SPLIT
    half = row_size // CORES
    queries = SPLIT * cols
    keys_count = col_size * cols
    depth = queries // CORES
    part = own_rows * cols

    send, spread = pl.pallas_call(
        functools.partial(norm_kernel, rows, cols),
        out_shape=(
            jax.ShapeDtypeStruct((col_size, part + depth, width), BF16),
            jax.ShapeDtypeStruct((half, rows, width), BF16),
        ),
        in_specs=[VMEM, VMEM, VMEM],
        out_specs=(VMEM, VMEM),
    )(pair.reshape(rows * cols, width), w_bias.T, token_mask[None])

    same_core = [[CORES * n + core for n in range(half)] for core in range(CORES)]
    bias = lax.all_to_all(spread, "row", 0, 0, axis_index_groups=same_core, tiled=True)

    send = pl.pallas_call(
        pack_kernel,
        out_shape=jax.ShapeDtypeStruct(send.shape, BF16),
        in_specs=[VMEM, ANY],
        out_specs=ANY,
        scratch_shapes=[pltpu.SemaphoreType.DMA((col_size,))],
        input_output_aliases={1: 0},
    )(bias.reshape(SPLIT, depth, width), send)
    block = lax.all_to_all(send, "col", 0, 0, tiled=True)

    swap = [(r, r ^ 1) for r in range(row_size)]
    other = lax.ppermute(block[:, part:], "row", swap)

    made = pl.pallas_call(
        functools.partial(project_kernel, heads, cols, own_rows),
        out_shape=jax.ShapeDtypeStruct((own_rows + 1, keys_count + queries, 2 * width), BF16),
        in_specs=[VMEM, VMEM, VMEM],
        out_specs=VMEM,
        compiler_params=pltpu.CompilerParams(vmem_limit_bytes=16 << 20),
    )(block, w_proj, w_out)

    answer = pl.pallas_call(
        functools.partial(attend_kernel, heads, cols),
        out_shape=jax.ShapeDtypeStruct((SPLIT, own_rows, cols, width), BF16),
        in_specs=[VMEM, VMEM, VMEM],
        out_specs=VMEM,
        scratch_shapes=[pltpu.VMEM((heads, SPLIT, CORES, depth // SPLIT, keys_count), F32)],
        compiler_params=pltpu.CompilerParams(vmem_limit_bytes=16 << 20),
    )(block, other, made)

    near = [[SPLIT * g + m for m in range(SPLIT)] for g in range(col_size // SPLIT)]
    back = lax.all_to_all(answer, "col", 0, 0, axis_index_groups=near, tiled=True)
    return back.reshape(rows, cols, width)


def solution(mesh):
    in_specs = (P("row", "col", None), P(), P(), P(), P("col"))
    out_specs = P("row", "col", None)
    body = functools.partial(on_device, row_size=mesh.shape["row"], col_size=mesh.shape["col"])
    return jax.shard_map(body, mesh=mesh, in_specs=in_specs, out_specs=out_specs, check_vma=False)
```

time: 76.4 us -> 71 us (0.929)
  blocking collectives: 34.6 us -> 55.3 us
  starting transfers between devices: 19.5 us -> 6.32 us
  waiting for transfers between devices: 9.79 us -> 0.62 us
  local copies, waits for them, and re-layouts: 2.8 us -> 0.68 us
  Pallas kernels: 8.67 us -> 7.36 us
    all_to_all x0 -> x1, blocking collectives: none -> 22.4 us  [on_device(): lax.all_to_all(spread, 'row', 0, 0, axis_index_groups=same_core, tiled=True)]
    all_to_all x1 -> x0, starting transfers between devices: 13.6 us -> none  [on_device(): lax.all_to_all(spread, 'row', 0, 0, axis_index_groups=same_core, tiled=True)]
    all_to_all x1 -> x0, waiting for transfers between devices: 8.76 us -> none  [on_device(): lax.all_to_all(spread, 'row', 0, 0, axis_index_groups=same_core, tiled=True)]
    all_to_all x1, blocking collectives: 26.5 us -> 24.9 us  [on_device(): block = lax.all_to_all(send, 'col', 0, 0, tiled=True)]
    unnamed x10 -> x5, local copies, waits for them, and re-layouts: 2.08 us -> 0.66 us
    pallas_call x3 -> x4, Pallas kernels: 8.67 us -> 7.36 us  [the longest x1 3.06 us: on_device(): pl.pallas_call(functools.partial(attend_kernel, heads, cols), out_shape=j...]
  transfers between devices with their start and end apart: 2 -> 1, of which waited for: 2 -> 1; matrix products, arithmetic and copies ran while one was open for 0% -> 0% of each run, Pallas kernels for 0% -> 1%
where the time goes in v2:
time: 71 us; the launch traced here: 70.3 us
  blocking collectives  55.3 us (78%)
  Pallas kernels  7.36 us (10%)
  starting transfers between devices  6.32 us (9%)
    all_to_all x1, blocking collectives, on_device(): block = lax.all_to_all(send, 'col', 0, 0, tiled=True)  24.9 us
    all_to_all x1, blocking collectives, on_device(): lax.all_to_all(spread, 'row', 0, 0, axis_index_groups=same_core, tiled=True)  22.4 us
    all_to_all x1, blocking collectives, on_device(): lax.all_to_all(answer, 'col', 0, 0, axis_index_groups=near, tiled=True)  7.93 us
    ppermute x1, starting transfers between devices, on_device(): other = lax.ppermute(block[:, part:], 'row', swap)  6.32 us
    pallas_call x1, Pallas kernels, on_device(): pl.pallas_call(functools.partial(attend_kernel, heads, cols), out_shape=j...  3.06 us
    pallas_call x1, Pallas kernels, on_device(): pl.pallas_call(functools.partial(norm_kernel, rows, cols), out_shape=(jax...  2.05 us
    pallas_call x1, Pallas kernels, on_device(): pl.pallas_call(pack_kernel, out_shape=jax.ShapeDtypeStruct(send.shape, BF...  1.76 us
  transfers between devices with their start and end apart: 1, of which 1 were waited for; matrix products, arithmetic and copies ran while one was open for 0% of the time, Pallas kernels for 1%

profile of v2, /device:TPU:1, one launch (start us, length us, event | category | flops | bytes accessed | tf_op | source)
XLA Modules:
  0.0 70.3 jit_solution(3005755748270454292)
XLA Ops:
  0.0 2.1 %shard_map.55 = (bf16[16,192,128]{2,1,0:T(8,128)(2,1)}, bf16[16,16,128]{2,1,0:T(8,128)(2,1)}) custom-call(bf16[512,128]{1,0:T(8,128)(2,1)} %bitcast.7, bf16[4,128]{1,0:T(4,128)(2,1)} %bitcast.8, s32[1,32]{1,0:T(1,128)} %bitcast.9), custom_call_target="tpu_custom_call" | custom-call | tf_op jit(solution)/shard_map/pallas_call | solution.py:156
  2.1 22.4 %all_to_all.15 = bf16[16,16,128]{2,1,0:T(8,128)(2,1)} all-to-all(bf16[16,16,128]{2,1,0:T(8,128)(2,1)} %get-tuple-element.7), channel_id=1, replica_groups={{0,32,64,96,128,160,192,224,256,288,320,352,384,416,448,480},{16,48,80,..., dimensions={0} | all-to-all | bytes 131072 | tf_op jit(solution)/shard_map/all_to_all | solution.py:167
  24.5 0.0 copy-start
  24.5 0.0 copy-start.1
  24.5 1.8 %shard_map.56 = bf16[16,192,128]{2,1,0:T(8,128)(2,1)} custom-call(bf16[4,64,128]{2,1,0:T(8,128)(2,1)} %bitcast.6, bf16[16,192,128]{2,1,0:T(8,128)(2,1)} %get-tuple-element.8.half_ref), custom_call_target="tpu_custom_call", output_to_operand_aliasing={{}: (1, {})} | custom-call | tf_op jit(solution)/shard_map/pallas_call | solution.py:169
  26.2 24.9 %all_to_all.16.block_ref = bf16[16,192,128]{2,1,0:T(8,128)(2,1)S(1)} all-to-all(bf16[16,192,128]{2,1,0:T(8,128)(2,1)} %shard_map.56), channel_id=1, replica_groups=mesh['row'=32,'col'=16] {'col'}, dimensions={0} | all-to-all | bytes 1572864 | tf_op jit(solution)/shard_map/all_to_all | solution.py:177
  51.2 6.3 %collective-permute-start = (bf16[16,64,128]{2,1,0:T(8,128)(2,1)S(1)}, bf16[16,64,128]{2,1,0:T(8,128)(2,1)S(1)}, u32[]{:S(2)}, u32[]{:S(2)}) collective-permute-start(bf16[16,64,128]{2,1,0:T(8,128)(2,1)S(1)} %slice.4), channel_id=1, source_target_pairs={{0,16},{16,0},{32,48},{48,32},{64,80},{80,64},{96,112},{112,96},{1... | collective-permute-start | bytes 786440 | tf_op jit(solution)/shard_map/ppermute | solution.py:180
  57.5 0.0 copy-done
  57.5 0.0 copy-done.1
  57.5 0.5 shard_map.57.made_ref
  58.0 0.6 collective-permute-done.other_ref
  58.7 3.1 %shard_map.58 = bf16[4,4,32,128]{3,2,1,0:T(8,128)(2,1)S(1)} custom-call(bf16[16,192,128]{2,1,0:T(8,128)(2,1)S(1)} %all_to_all.16.block_ref, bf16[16,64,128]{2,1,0:T(8,128)(2,1)S(1)} %collective-permute-done.other_ref, bf16[5,640,256]{2,1,0:T(8,128)(2,1)S(1)} %shard_map.57.made_ref), custom_call_target="tpu_custom_call" | custom-call | tf_op jit(solution)/shard_map/pallas_call | solution.py:190
  61.7 7.9 %all_to_all.17 = bf16[4,4,32,128]{3,2,1,0:T(8,128)(2,1)S(1)} all-to-all(bf16[4,4,32,128]{3,2,1,0:T(8,128)(2,1)S(1)} %shard_map.58), channel_id=1, replica_groups={{0,1,2,3},{4,5,6,7},{8,9,10,11},{12,13,14,15},{16,17,18,19},{20,21,22,2..., dimensions={0} | all-to-all | bytes 262144 | tf_op jit(solution)/shard_map/all_to_all | solution.py:200
  69.7 0.7 copy.9
  (1 shorter events, 0.0 us)
Async XLA Ops:
  24.5 33.1 %copy-start = (bf16[128,512]{1,0:T(8,128)(2,1)S(1)}, bf16[128,512]{1,0:T(8,128)(2,1)}, u32[]{:S(2)}) copy-start(bf16[128,512]{1,0:T(8,128)(2,1)} %w_proj_ref.1) | copy-start | bytes 393220
  24.5 33.1 %copy-start.1 = (bf16[128,128]{1,0:T(8,128)(2,1)S(1)}, bf16[128,128]{1,0:T(8,128)(2,1)}, u32[]{:S(2)}) copy-start(bf16[128,128]{1,0:T(8,128)(2,1)} %w_out_ref.1) | copy-start | bytes 98308
  51.2 7.5 %collective-permute-start = (bf16[16,64,128]{2,1,0:T(8,128)(2,1)S(1)}, bf16[16,64,128]{2,1,0:T(8,128)(2,1)S(1)}, u32[]{:S(2)}, u32[]{:S(2)}) collective-permute-start(bf16[16,64,128]{2,1,0:T(8,128)(2,1)S(1)} %slice.4), channel_id=1, source_target_pairs={{0,16},{16,0},{32,48},{48,32},{64,80},{80,64},{96,112},{112,96},{1... | collective-permute-start | bytes 786440 | tf_op jit(solution)/shard_map/ppermute | solution.py:180

commit v3 on v2

--- a/solution.py
+++ b/solution.py
@@ -16,6 +16,14 @@
 CORES = 2
 
 
+def joined(group, sub):
+    return sub // 2 * 2 * SPLIT + group * 2 + sub % 2
+
+
+def sub_of(col):
+    return col // (2 * SPLIT) * 2 + col % 2
+
+
 def norm_rows(values):
     center = jnp.mean(values, axis=-1, keepdims=True)
     shifted = values - center
@@ -28,7 +36,7 @@
     width = normed.shape[1]
     part = normed.shape[0] // SPLIT
     for member in range(send_ref.shape[0]):
-        sub = member % SPLIT
+        sub = sub_of(member)
         send_ref[member, 0:part] = normed[sub * part : (sub + 1) * part]
 
     heads = w_bias_ref.shape[0]
@@ -51,37 +59,22 @@
         spread_ref[member] = bias
 
 
-def pack_kernel(bias_ref, half_ref, send_ref, done):
-    del half_ref
-    members, chunk, _ = send_ref.shape
-    depth = bias_ref.shape[1]
-    copies = [
-        pltpu.make_async_copy(
-            bias_ref.at[member // SPLIT],
-            send_ref.at[member, pl.ds(chunk - depth, depth)],
-            done.at[member],
-        )
-        for member in range(members)
-    ]
-    for copy in copies:
-        copy.start()
-    for copy in copies:
-        copy.wait()
-
-
 def project_kernel(heads, cols, own_rows, block_ref, w_proj_ref, w_out_ref, made_ref):
     members, _, width = block_ref.shape
     head_size = width // heads
     keys_count = members * cols
     queries = SPLIT * cols
-    first = lax.axis_index("col") // SPLIT * SPLIT
+    first = lax.axis_index("col") // 2 % SPLIT * 2
     for row in range(own_rows):
         entries = block_ref[:, row * cols : (row + 1) * cols].reshape(keys_count, width)
         made_ref[row, :keys_count] = jnp.dot(
             entries, w_proj_ref[:, width : 3 * width], preferred_element_type=F32
         ).astype(BF16)
-        asking = block_ref[pl.ds(first, SPLIT), row * cols : (row + 1) * cols]
-        asking = asking.reshape(queries, width)
+        asking = [
+            block_ref[pl.ds(first + start, 2), row * cols : (row + 1) * cols]
+            for start in (0, 2 * SPLIT)
+        ]
+        asking = jnp.concatenate(asking, axis=0).reshape(queries, width)
         query = jnp.dot(asking, w_proj_ref[:, :width], preferred_element_type=F32)
         made_ref[row, keys_count:, :width] = (query * head_size ** (-0.5)).astype(BF16)
         gates = jnp.dot(asking, w_proj_ref[:, 3 * width :], preferred_element_type=F32)
@@ -166,14 +159,9 @@
     same_core = [[CORES * n + core for n in range(half)] for core in range(CORES)]
     bias = lax.all_to_all(spread, "row", 0, 0, axis_index_groups=same_core, tiled=True)
 
-    send = pl.pallas_call(
-        pack_kernel,
-        out_shape=jax.ShapeDtypeStruct(send.shape, BF16),
-        in_specs=[VMEM, ANY],
-        out_specs=ANY,
-        scratch_shapes=[pltpu.SemaphoreType.DMA((col_size,))],
-        input_output_aliases={1: 0},
-    )(bias.reshape(SPLIT, depth, width), send)
+    bias = bias.reshape(2, SPLIT, 2, rows, width).transpose(1, 0, 2, 3, 4).reshape(SPLIT, 1, depth, width)
+    bias = jnp.broadcast_to(bias[None], (2, SPLIT, 2, depth, width)).reshape(col_size, depth, width)
+    send = lax.dynamic_update_slice(send, bias, (0, part, 0))
     block = lax.all_to_all(send, "col", 0, 0, tiled=True)
 
     swap = [(r, r ^ 1) for r in range(row_size)]
@@ -196,9 +184,9 @@
         compiler_params=pltpu.CompilerParams(vmem_limit_bytes=16 << 20),
     )(block, other, made)
 
-    near = [[SPLIT * g + m for m in range(SPLIT)] for g in range(col_size // SPLIT)]
-    back = lax.all_to_all(answer, "col", 0, 0, axis_index_groups=near, tiled=True)
-    return back.reshape(rows, cols, width)
+    near = [[joined(group, sub) for sub in range(SPLIT)] for group in range(SPLIT)]
+    answer = answer.reshape(rows, cols, width)
+    return lax.all_to_all(answer, "col", 0, 0, axis_index_groups=near, tiled=True)
 
 
 def solution(mesh):

time: 71 us -> 69.2 us (0.975)
  Pallas kernels: 7.36 us -> 5.61 us
  local copies, waits for them, and re-layouts: 0.68 us -> 1.52 us
    pallas_call x1 -> x0, Pallas kernels: 1.76 us -> none  [on_device(): pl.pallas_call(pack_kernel, out_shape=jax.ShapeDtypeStruct(send.shape, BF...]
    dynamic_update_slice x0 -> x1, local copies, waits for them, and re-layouts: none -> 0.79 us  [on_device(): send = lax.dynamic_update_slice(send, bias, (0, part, 0))]
where the time goes in v3:
time: 69.2 us; the launch traced here: 68.8 us
  blocking collectives  54.7 us (79%)
  starting transfers between devices  6.32 us (9%)
  Pallas kernels  5.61 us (8%)
  local copies, waits for them, and re-layouts  1.52 us (2%)
    all_to_all x1, blocking collectives, on_device(): block = lax.all_to_all(send, 'col', 0, 0, tiled=True)  24.9 us
    all_to_all x1, blocking collectives, on_device(): lax.all_to_all(spread, 'row', 0, 0, axis_index_groups=same_core, tiled=True)  22.4 us
    all_to_all x1, blocking collectives, on_device(): lax.all_to_all(answer, 'col', 0, 0, axis_index_groups=near, tiled=True)  7.36 us
    ppermute x1, starting transfers between devices, on_device(): other = lax.ppermute(block[:, part:], 'row', swap)  6.32 us
    pallas_call x1, Pallas kernels, on_device(): pl.pallas_call(functools.partial(attend_kernel, heads, cols), out_shape=j...  3.06 us
    pallas_call x1, Pallas kernels, on_device(): pl.pallas_call(functools.partial(norm_kernel, rows, cols), out_shape=(jax...  2.05 us
  transfers between devices with their start and end apart: 1, of which 1 were waited for; matrix products, arithmetic and copies ran while one was open for 0% of the time, Pallas kernels for 1%

profile of v3, /device:TPU:1, one launch (start us, length us, event | category | flops | bytes accessed | tf_op | source)
XLA Modules:
  0.0 68.8 jit_solution(16056683423062244158)
XLA Ops:
  0.0 2.1 %shard_map.55 = (bf16[16,192,128]{2,1,0:T(8,128)(2,1)}, bf16[16,16,128]{2,1,0:T(8,128)(2,1)}) custom-call(bf16[512,128]{1,0:T(8,128)(2,1)} %bitcast.13, bf16[4,128]{1,0:T(4,128)(2,1)} %bitcast.14, s32[1,32]{1,0:T(1,128)} %bitcast.15), custom_call_target="tpu_custom_call" | custom-call | tf_op jit(solution)/shard_map/pallas_call | solution.py:149
  2.1 0.0 copy-start
  2.1 0.0 copy-start.1
  2.1 22.4 %all_to_all.15 = bf16[16,16,128]{2,1,0:T(8,128)(2,1)S(1)} all-to-all(bf16[16,16,128]{2,1,0:T(8,128)(2,1)} %get-tuple-element.8), channel_id=1, replica_groups={{0,32,64,96,128,160,192,224,256,288,320,352,384,416,448,480},{16,48,80,..., dimensions={0} | all-to-all | bytes 131072 | tf_op jit(solution)/shard_map/all_to_all | solution.py:160
  24.6 0.8 %constant_dynamic-update-slice_fusion = bf16[16,192,128]{2,1,0:T(8,128)(2,1)} fusion(bf16[16,192,128]{2,1,0:T(8,128)(2,1)} %get-tuple-element.7, bf16[16,64,128]{2,1,0:T(8,128)(2,1)S(1)} %bitcast.10), kind=kLoop, calls=%fused_computation | loop fusion | bytes 524288 | tf_op jit(solution)/shard_map/dynamic_update_slice | solution.py:164
  25.3 24.9 %all_to_all.16.block_ref = bf16[16,192,128]{2,1,0:T(8,128)(2,1)S(1)} all-to-all(bf16[16,192,128]{2,1,0:T(8,128)(2,1)} %constant_dynamic-update-slice_fusion), channel_id=1, replica_groups=mesh['row'=32,'col'=16] {'col'}, dimensions={0} | all-to-all | bytes 1572864 | tf_op jit(solution)/shard_map/all_to_all | solution.py:165
  50.3 6.3 %collective-permute-start = (bf16[16,64,128]{2,1,0:T(8,128)(2,1)S(1)}, bf16[16,64,128]{2,1,0:T(8,128)(2,1)S(1)}, u32[]{:S(2)}, u32[]{:S(2)}) collective-permute-start(bf16[16,64,128]{2,1,0:T(8,128)(2,1)S(1)} %slice.4), channel_id=1, source_target_pairs={{0,16},{16,0},{32,48},{48,32},{64,80},{80,64},{96,112},{112,96},{1... | collective-permute-start | bytes 786440 | tf_op jit(solution)/shard_map/ppermute | solution.py:168
  56.6 0.0 copy-done
  56.6 0.0 copy-done.1
  56.6 0.5 shard_map.56.made_ref
  57.1 0.6 collective-permute-done.other_ref
  57.8 3.1 %shard_map.57 = bf16[4,4,32,128]{3,2,1,0:T(8,128)(2,1)S(1)} custom-call(bf16[16,192,128]{2,1,0:T(8,128)(2,1)S(1)} %all_to_all.16.block_ref, bf16[16,64,128]{2,1,0:T(8,128)(2,1)S(1)} %collective-permute-done.other_ref, bf16[5,640,256]{2,1,0:T(8,128)(2,1)S(1)} %shard_map.56.made_ref), custom_call_target="tpu_custom_call" | custom-call | tf_op jit(solution)/shard_map/pallas_call | solution.py:178
  60.8 7.4 %all_to_all.17 = bf16[16,32,128]{2,1,0:T(8,128)(2,1)S(1)} all-to-all(bf16[16,32,128]{2,1,0:T(8,128)(2,1)S(1)} %bitcast.9), channel_id=1, replica_groups={{0,1,8,9},{2,3,10,11},{4,5,12,13},{6,7,14,15},{16,17,24,25},{18,19,26,2..., dimensions={0} | all-to-all | bytes 262144 | tf_op jit(solution)/shard_map/all_to_all | solution.py:189
  68.2 0.7 copy.9
  (3 shorter events, 0.1 us)
Async XLA Ops:
  2.1 54.6 %copy-start = (bf16[128,512]{1,0:T(8,128)(2,1)S(1)}, bf16[128,512]{1,0:T(8,128)(2,1)}, u32[]{:S(2)}) copy-start(bf16[128,512]{1,0:T(8,128)(2,1)} %w_proj_ref.1) | copy-start | bytes 393220
  2.1 54.6 %copy-start.1 = (bf16[128,128]{1,0:T(8,128)(2,1)S(1)}, bf16[128,128]{1,0:T(8,128)(2,1)}, u32[]{:S(2)}) copy-start(bf16[128,128]{1,0:T(8,128)(2,1)} %w_out_ref.1) | copy-start | bytes 98308
  50.3 7.5 %collective-permute-start = (bf16[16,64,128]{2,1,0:T(8,128)(2,1)S(1)}, bf16[16,64,128]{2,1,0:T(8,128)(2,1)S(1)}, u32[]{:S(2)}, u32[]{:S(2)}) collective-permute-start(bf16[16,64,128]{2,1,0:T(8,128)(2,1)S(1)} %slice.4), channel_id=1, source_target_pairs={{0,16},{16,0},{32,48},{48,32},{64,80},{80,64},{96,112},{112,96},{1... | collective-permute-start | bytes 786440 | tf_op jit(solution)/shard_map/ppermute | solution.py:168

commit v4 on v3

--- a/solution.py
+++ b/solution.py
@@ -10,7 +10,6 @@
 F32 = jnp.float32
 BF16 = jnp.bfloat16
 VMEM = pl.BlockSpec(memory_space=pltpu.VMEM)
-ANY = pl.BlockSpec(memory_space=pl.ANY)
 
 SPLIT = 4
 CORES = 2
@@ -91,6 +90,19 @@
     part = block_ref.shape[1] - depth
     parity = lax.axis_index("row") % CORES
 
+    lane_head = lax.broadcasted_iota(jnp.int32, (1, width), 1) // (width // heads)
+
+    def products(row):
+        query = made_ref[row, keys_count:, :width].astype(F32)
+        wide = [jnp.where(lane_head == head, query, 0.0).astype(BF16) for head in range(heads)]
+        return lax.dot_general(
+            jnp.concatenate(wide, axis=0),
+            made_ref[row, :keys_count, :width],
+            (((1,), (1,)), ((), ())),
+            preferred_element_type=F32,
+        )
+
+    ahead = products(0)
     segment = lax.broadcasted_iota(jnp.int32, (1, width), 1) // cols
     for turn in range(members // group):
         for source in range(CORES):
@@ -108,32 +120,31 @@
                 value = value.reshape(SPLIT, depth // SPLIT, width)
                 bias_ref[head, :, core, :, turn * width : (turn + 1) * width] = value
 
-    lane_head = lax.broadcasted_iota(jnp.int32, (1, width), 1) // (width // heads)
     w_out = made_ref[own_rows, :width, :width]
     ones = jnp.ones((keys_count, width), BF16)
+    gated = []
     for row in range(own_rows):
-        query = made_ref[row, keys_count:, :width].astype(F32)
+        scores = ahead
+        if row + 1 < own_rows:
+            ahead = products(row + 1)
+        weights = []
+        for head in range(heads):
+            value = scores[head * queries : (head + 1) * queries]
+            value = value + bias_ref[head].reshape(queries, keys_count)
+            top = jnp.max(value, axis=-1, keepdims=True)
+            weights.append(jnp.exp(value - top).astype(BF16))
         values = jnp.concatenate([made_ref[row, :keys_count, width:], ones], axis=1)
         above = jnp.zeros((queries, width), F32)
         below = jnp.zeros((queries, width), F32)
         for head in range(heads):
-            chosen = jnp.where(lane_head == head, query, 0.0).astype(BF16)
-            scores = lax.dot_general(
-                chosen,
-                made_ref[row, :keys_count, :width],
-                (((1,), (1,)), ((), ())),
-                preferred_element_type=F32,
-            )
-            scores = scores + bias_ref[head].reshape(queries, keys_count)
-            top = jnp.max(scores, axis=-1, keepdims=True)
-            weights = jnp.exp(scores - top).astype(BF16)
-            sums = jnp.dot(weights, values, preferred_element_type=F32)
+            sums = jnp.dot(weights[head], values, preferred_element_type=F32)
             above = jnp.where(lane_head == head, sums[:, :width], above)
             below = jnp.where(lane_head == head, sums[:, width:], below)
         gates = made_ref[row, keys_count:, width:].astype(F32)
-        gated = (above / below * jax.nn.sigmoid(gates)).astype(BF16)
-        result = jnp.dot(gated, w_out, preferred_element_type=F32).astype(BF16)
-        out_ref[:, row] = result.reshape(SPLIT, cols, width)
+        gated.append((above / below * jax.nn.sigmoid(gates)).astype(BF16))
+    result = jnp.dot(jnp.concatenate(gated, axis=0), w_out, preferred_element_type=F32).astype(BF16)
+    for row in range(own_rows):
+        out_ref[:, row] = result[row * queries : (row + 1) * queries].reshape(SPLIT, cols, width)
 
 
 def on_device(pair, w_proj, w_bias, w_out, token_mask, *, row_size, col_size):

time: 69.2 us -> 68.1 us (0.984)
  Pallas kernels: 5.61 us -> 4.54 us
    pallas_call x1, Pallas kernels: 3.06 us -> 1.99 us  [on_device(): pl.pallas_call(functools.partial(attend_kernel, heads, cols), out_shape=j...]
where the time goes in v4:
time: 68.1 us; the launch traced here: 67.8 us
  blocking collectives  54.7 us (80%)
  starting transfers between devices  6.32 us (9%)
  Pallas kernels  4.54 us (7%)
  local copies, waits for them, and re-layouts  1.52 us (2%)
    all_to_all x1, blocking collectives, on_device(): block = lax.all_to_all(send, 'col', 0, 0, tiled=True)  24.9 us
    all_to_all x1, blocking collectives, on_device(): lax.all_to_all(spread, 'row', 0, 0, axis_index_groups=same_core, tiled=True)  22.4 us
    all_to_all x1, blocking collectives, on_device(): lax.all_to_all(answer, 'col', 0, 0, axis_index_groups=near, tiled=True)  7.35 us
    ppermute x1, starting transfers between devices, on_device(): other = lax.ppermute(block[:, part:], 'row', swap)  6.32 us
    pallas_call x1, Pallas kernels, on_device(): pl.pallas_call(functools.partial(norm_kernel, rows, cols), out_shape=(jax...  2.05 us
    pallas_call x1, Pallas kernels, on_device(): pl.pallas_call(functools.partial(attend_kernel, heads, cols), out_shape=j...  1.99 us
  transfers between devices with their start and end apart: 1, of which 1 were waited for; matrix products, arithmetic and copies ran while one was open for 0% of the time, Pallas kernels for 1%

profile of v4, /device:TPU:1, one launch (start us, length us, event | category | flops | bytes accessed | tf_op | source)
XLA Modules:
  0.0 67.8 jit_solution(8356829293383302068)
XLA Ops:
  0.0 2.1 %shard_map.55 = (bf16[16,192,128]{2,1,0:T(8,128)(2,1)}, bf16[16,16,128]{2,1,0:T(8,128)(2,1)}) custom-call(bf16[512,128]{1,0:T(8,128)(2,1)} %bitcast.13, bf16[4,128]{1,0:T(4,128)(2,1)} %bitcast.14, s32[1,32]{1,0:T(1,128)} %bitcast.15), custom_call_target="tpu_custom_call" | custom-call | tf_op jit(solution)/shard_map/pallas_call | solution.py:160
  2.1 0.0 copy-start
  2.1 0.0 copy-start.1
  2.1 22.4 %all_to_all.15 = bf16[16,16,128]{2,1,0:T(8,128)(2,1)S(1)} all-to-all(bf16[16,16,128]{2,1,0:T(8,128)(2,1)} %get-tuple-element.8), channel_id=1, replica_groups={{0,32,64,96,128,160,192,224,256,288,320,352,384,416,448,480},{16,48,80,..., dimensions={0} | all-to-all | bytes 131072 | tf_op jit(solution)/shard_map/all_to_all | solution.py:171
  24.6 0.8 %constant_dynamic-update-slice_fusion = bf16[16,192,128]{2,1,0:T(8,128)(2,1)} fusion(bf16[16,192,128]{2,1,0:T(8,128)(2,1)} %get-tuple-element.7, bf16[16,64,128]{2,1,0:T(8,128)(2,1)S(1)} %bitcast.10), kind=kLoop, calls=%fused_computation | loop fusion | bytes 524288 | tf_op jit(solution)/shard_map/dynamic_update_slice | solution.py:175
  25.3 24.9 %all_to_all.16.block_ref = bf16[16,192,128]{2,1,0:T(8,128)(2,1)S(1)} all-to-all(bf16[16,192,128]{2,1,0:T(8,128)(2,1)} %constant_dynamic-update-slice_fusion), channel_id=1, replica_groups=mesh['row'=32,'col'=16] {'col'}, dimensions={0} | all-to-all | bytes 1572864 | tf_op jit(solution)/shard_map/all_to_all | solution.py:176
  50.3 6.3 %collective-permute-start = (bf16[16,64,128]{2,1,0:T(8,128)(2,1)S(1)}, bf16[16,64,128]{2,1,0:T(8,128)(2,1)S(1)}, u32[]{:S(2)}, u32[]{:S(2)}) collective-permute-start(bf16[16,64,128]{2,1,0:T(8,128)(2,1)S(1)} %slice.4), channel_id=1, source_target_pairs={{0,16},{16,0},{32,48},{48,32},{64,80},{80,64},{96,112},{112,96},{1... | collective-permute-start | bytes 786440 | tf_op jit(solution)/shard_map/ppermute | solution.py:179
  56.6 0.0 copy-done
  56.6 0.0 copy-done.1
  56.6 0.5 shard_map.56.made_ref
  57.1 0.6 collective-permute-done.other_ref
  57.8 2.0 %shard_map.57 = bf16[4,4,32,128]{3,2,1,0:T(8,128)(2,1)S(1)} custom-call(bf16[16,192,128]{2,1,0:T(8,128)(2,1)S(1)} %all_to_all.16.block_ref, bf16[16,64,128]{2,1,0:T(8,128)(2,1)S(1)} %collective-permute-done.other_ref, bf16[5,640,256]{2,1,0:T(8,128)(2,1)S(1)} %shard_map.56.made_ref), custom_call_target="tpu_custom_call" | custom-call | tf_op jit(solution)/shard_map/pallas_call | solution.py:189
  59.8 7.4 %all_to_all.17 = bf16[16,32,128]{2,1,0:T(8,128)(2,1)S(1)} all-to-all(bf16[16,32,128]{2,1,0:T(8,128)(2,1)S(1)} %bitcast.9), channel_id=1, replica_groups={{0,1,8,9},{2,3,10,11},{4,5,12,13},{6,7,14,15},{16,17,24,25},{18,19,26,2..., dimensions={0} | all-to-all | bytes 262144 | tf_op jit(solution)/shard_map/all_to_all | solution.py:200
  67.1 0.7 copy.9
  (3 shorter events, 0.1 us)
Async XLA Ops:
  2.1 54.6 %copy-start = (bf16[128,512]{1,0:T(8,128)(2,1)S(1)}, bf16[128,512]{1,0:T(8,128)(2,1)}, u32[]{:S(2)}) copy-start(bf16[128,512]{1,0:T(8,128)(2,1)} %w_proj_ref.1) | copy-start | bytes 393220
  2.1 54.6 %copy-start.1 = (bf16[128,128]{1,0:T(8,128)(2,1)S(1)}, bf16[128,128]{1,0:T(8,128)(2,1)}, u32[]{:S(2)}) copy-start(bf16[128,128]{1,0:T(8,128)(2,1)} %w_out_ref.1) | copy-start | bytes 98308
  50.3 7.5 %collective-permute-start = (bf16[16,64,128]{2,1,0:T(8,128)(2,1)S(1)}, bf16[16,64,128]{2,1,0:T(8,128)(2,1)S(1)}, u32[]{:S(2)}, u32[]{:S(2)}) collective-permute-start(bf16[16,64,128]{2,1,0:T(8,128)(2,1)S(1)} %slice.4), channel_id=1, source_target_pairs={{0,16},{16,0},{32,48},{48,32},{64,80},{80,64},{96,112},{112,96},{1... | collective-permute-start | bytes 786440 | tf_op jit(solution)/shard_map/ppermute | solution.py:179

commit v5 on v4

--- a/solution.py
+++ b/solution.py
@@ -30,22 +30,24 @@
     return (shifted * lax.rsqrt(spread + 1e-05)).astype(BF16)
 
 
-def norm_kernel(rows, cols, pair_ref, w_bias_ref, mask_ref, send_ref, spread_ref):
+def norm_kernel(pair_ref, send_ref, normed_ref):
     normed = norm_rows(pair_ref[...].astype(F32))
-    width = normed.shape[1]
+    normed_ref[...] = normed
     part = normed.shape[0] // SPLIT
     for member in range(send_ref.shape[0]):
         sub = sub_of(member)
         send_ref[member, 0:part] = normed[sub * part : (sub + 1) * part]
 
-    heads = w_bias_ref.shape[0]
+
+def bias_kernel(rows, cols, normed_ref, w_bias_ref, mask_ref, spread_ref):
+    heads, width = w_bias_ref.shape
     head_of_row = lax.broadcasted_iota(jnp.int32, (width, width), 0) // cols
     w_bias = w_bias_ref[...].astype(F32)
     wide = jnp.zeros((width, width), F32)
     for head in range(heads):
         wide = jnp.where(head_of_row == head, w_bias[head : head + 1], wide)
     product = lax.dot_general(
-        normed, wide.astype(BF16), (((1,), (1,)), ((), ())), preferred_element_type=F32
+        normed_ref[...], wide.astype(BF16), (((1,), (1,)), ((), ())), preferred_element_type=F32
     )
     column = lax.broadcasted_iota(jnp.int32, product.shape, 0) % cols
     place = lax.broadcasted_iota(jnp.int32, product.shape, 1) % cols
@@ -58,7 +60,20 @@
         spread_ref[member] = bias
 
 
-def project_kernel(heads, cols, own_rows, block_ref, w_proj_ref, w_out_ref, made_ref):
+def products(heads, keys_count, made_ref, row):
+    width = made_ref.shape[2] // 2
+    lane_head = lax.broadcasted_iota(jnp.int32, (1, width), 1) // (width // heads)
+    query = made_ref[row, keys_count:, :width].astype(F32)
+    wide = [jnp.where(lane_head == head, query, 0.0).astype(BF16) for head in range(heads)]
+    return lax.dot_general(
+        jnp.concatenate(wide, axis=0),
+        made_ref[row, :keys_count, :width],
+        (((1,), (1,)), ((), ())),
+        preferred_element_type=F32,
+    )
+
+
+def project_kernel(heads, cols, own_rows, block_ref, w_proj_ref, w_out_ref, made_ref, ahead_ref):
     members, _, width = block_ref.shape
     head_size = width // heads
     keys_count = members * cols
@@ -79,9 +94,10 @@
         gates = jnp.dot(asking, w_proj_ref[:, 3 * width :], preferred_element_type=F32)
         made_ref[row, keys_count:, width:] = gates.astype(BF16)
     made_ref[own_rows, :width, :width] = w_out_ref[...]
-
-
-def attend_kernel(heads, cols, block_ref, other_ref, made_ref, out_ref, bias_ref):
+    ahead_ref[...] = products(heads, keys_count, made_ref, 0)
+
+
+def attend_kernel(heads, cols, block_ref, other_ref, made_ref, ahead_ref, out_ref, bias_ref):
     members, depth, width = other_ref.shape
     own_rows = made_ref.shape[0] - 1
     queries = SPLIT * cols
@@ -92,17 +108,6 @@
 
     lane_head = lax.broadcasted_iota(jnp.int32, (1, width), 1) // (width // heads)
 
-    def products(row):
-        query = made_ref[row, keys_count:, :width].astype(F32)
-        wide = [jnp.where(lane_head == head, query, 0.0).astype(BF16) for head in range(heads)]
-        return lax.dot_general(
-            jnp.concatenate(wide, axis=0),
-            made_ref[row, :keys_count, :width],
-            (((1,), (1,)), ((), ())),
-            preferred_element_type=F32,
-        )
-
-    ahead = products(0)
     segment = lax.broadcasted_iota(jnp.int32, (1, width), 1) // cols
     for turn in range(members // group):
         for source in range(CORES):
@@ -124,9 +129,9 @@
     ones = jnp.ones((keys_count, width), BF16)
     gated = []
     for row in range(own_rows):
-        scores = ahead
+        scores = ahead_ref if row == 0 else ahead
         if row + 1 < own_rows:
-            ahead = products(row + 1)
+            ahead = products(heads, keys_count, made_ref, row + 1)
         weights = []
         for head in range(heads):
             value = scores[head * queries : (head + 1) * queries]
@@ -157,43 +162,58 @@
     depth = queries // CORES
     part = own_rows * cols
 
-    send, spread = pl.pallas_call(
-        functools.partial(norm_kernel, rows, cols),
+    send, normed = pl.pallas_call(
+        norm_kernel,
         out_shape=(
             jax.ShapeDtypeStruct((col_size, part + depth, width), BF16),
-            jax.ShapeDtypeStruct((half, rows, width), BF16),
+            jax.ShapeDtypeStruct((rows * cols, width), BF16),
+        ),
+        in_specs=[VMEM],
+        out_specs=(VMEM, VMEM),
+        compiler_params=pltpu.CompilerParams(vmem_limit_bytes=4 << 20),
+        cost_estimate=pl.CostEstimate(flops=1 << 30, bytes_accessed=16 << 20, transcendentals=0),
+    )(pair.reshape(rows * cols, width))
+    spread = pl.pallas_call(
+        functools.partial(bias_kernel, rows, cols),
+        out_shape=jax.ShapeDtypeStruct((half, rows, width), BF16),
+        in_specs=[VMEM, VMEM, VMEM],
+        out_specs=VMEM,
+        compiler_params=pltpu.CompilerParams(vmem_limit_bytes=4 << 20),
+    )(normed, w_bias.T, token_mask[None])
+
+    same_core = [
+        [CORES * joined(group, sub) + core for group in range(SPLIT) for sub in range(SPLIT)]
+        for core in range(CORES)
+    ]
+    bias = lax.all_to_all(spread, "row", 0, 0, axis_index_groups=same_core, tiled=True)
+
+    bias = bias.reshape(1, SPLIT, 1, depth, width)
+    bias = jnp.broadcast_to(bias, (2, SPLIT, 2, depth, width)).reshape(col_size, depth, width)
+    send = lax.dynamic_update_slice(send, bias, (0, part, 0))
+    block = lax.all_to_all(send, "col", 0, 0, tiled=True)
+
+    swap = [(r, r ^ 1) for r in range(row_size)]
+    other = lax.ppermute(block[:, part:], "row", swap)
+
+    made, ahead = pl.pallas_call(
+        functools.partial(project_kernel, heads, cols, own_rows),
+        out_shape=(
+            jax.ShapeDtypeStruct((own_rows + 1, keys_count + queries, 2 * width), BF16),
+            jax.ShapeDtypeStruct((heads * queries, keys_count), F32),
         ),
         in_specs=[VMEM, VMEM, VMEM],
         out_specs=(VMEM, VMEM),
-    )(pair.reshape(rows * cols, width), w_bias.T, token_mask[None])
-
-    same_core = [[CORES * n + core for n in range(half)] for core in range(CORES)]
-    bias = lax.all_to_all(spread, "row", 0, 0, axis_index_groups=same_core, tiled=True)
-
-    bias = bias.reshape(2, SPLIT, 2, rows, width).transpose(1, 0, 2, 3, 4).reshape(SPLIT, 1, depth, width)
-    bias = jnp.broadcast_to(bias[None], (2, SPLIT, 2, depth, width)).reshape(col_size, depth, width)
-    send = lax.dynamic_update_slice(send, bias, (0, part, 0))
-    block = lax.all_to_all(send, "col", 0, 0, tiled=True)
-
-    swap = [(r, r ^ 1) for r in range(row_size)]
-    other = lax.ppermute(block[:, part:], "row", swap)
-
-    made = pl.pallas_call(
-        functools.partial(project_kernel, heads, cols, own_rows),
-        out_shape=jax.ShapeDtypeStruct((own_rows + 1, keys_count + queries, 2 * width), BF16),
-        in_specs=[VMEM, VMEM, VMEM],
-        out_specs=VMEM,
-        compiler_params=pltpu.CompilerParams(vmem_limit_bytes=16 << 20),
+        compiler_params=pltpu.CompilerParams(vmem_limit_bytes=12 << 20),
     )(block, w_proj, w_out)
 
     answer = pl.pallas_call(
         functools.partial(attend_kernel, heads, cols),
         out_shape=jax.ShapeDtypeStruct((SPLIT, own_rows, cols, width), BF16),
-        in_specs=[VMEM, VMEM, VMEM],
+        in_specs=[VMEM, VMEM, VMEM, VMEM],
         out_specs=VMEM,
         scratch_shapes=[pltpu.VMEM((heads, SPLIT, CORES, depth // SPLIT, keys_count), F32)],
-        compiler_params=pltpu.CompilerParams(vmem_limit_bytes=16 << 20),
-    )(block, other, made)
+        compiler_params=pltpu.CompilerParams(vmem_limit_bytes=12 << 20),
+    )(block, other, made, ahead)
 
     near = [[joined(group, sub) for sub in range(SPLIT)] for group in range(SPLIT)]
     answer = answer.reshape(rows, cols, width)

time: 68.1 us -> 66.6 us (0.978)
  Pallas kernels: 4.54 us -> 3.09 us
    pallas_call x1 -> x2, Pallas kernels: 2.05 us -> 0.45 us  [the longest x1 0.23 us: on_device(): pl.pallas_call(norm_kernel, out_shape=(jax.ShapeDtypeStruct((col_size, pa...]
    unnamed x5 -> x11, local copies, waits for them, and re-layouts: 0.66 us -> 2.01 us
    dynamic_update_slice x1, local copies, waits for them, and re-layouts: 0.79 us -> 0.04 us  [on_device(): send = lax.dynamic_update_slice(send, bias, (0, part, 0))]
where the time goes in v5:
time: 66.6 us; the launch traced here: 66.3 us
  blocking collectives  54.3 us (82%)
  starting transfers between devices  6.22 us (9%)
  Pallas kernels  3.09 us (5%)
  local copies, waits for them, and re-layouts  2.11 us (3%)
    all_to_all x1, blocking collectives, on_device(): block = lax.all_to_all(send, 'col', 0, 0, tiled=True)  24.8 us
    all_to_all x1, blocking collectives, on_device(): lax.all_to_all(spread, 'row', 0, 0, axis_index_groups=same_core, tiled=True)  22.2 us
    all_to_all x1, blocking collectives, on_device(): lax.all_to_all(answer, 'col', 0, 0, axis_index_groups=near, tiled=True)  7.35 us
    ppermute x1, starting transfers between devices, on_device(): other = lax.ppermute(block[:, part:], 'row', swap)  6.22 us
    unnamed x11, local copies, waits for them, and re-layouts  2.01 us
    pallas_call x1, Pallas kernels, on_device(): pl.pallas_call(functools.partial(attend_kernel, heads, cols), out_shape=j...  2 us
  transfers between devices with their start and end apart: 1, of which 1 were waited for; matrix products, arithmetic and copies ran while one was open for 0% of the time, Pallas kernels for 1%

profile of v5, /device:TPU:1, one launch (start us, length us, event | category | flops | bytes accessed | tf_op | source)
XLA Modules:
  0.0 66.3 jit_solution(12022873819268920171)
XLA Ops:
  0.0 0.0 copy-start.4
  0.0 0.9 %copy-done.4 = bf16[16,32,128]{2,1,0:T(8,128)(2,1)S(1)} copy-done((bf16[16,32,128]{2,1,0:T(8,128)(2,1)S(1)}, bf16[16,32,128]{2,1,0:T(8,128)(2,1)}, u32[]{:S(2)}) %copy-start.4) | copy-done | bytes 131096
  0.9 0.0 copy-start.2
  0.9 0.0 copy-start.3
  0.9 0.2 shard_map.55
  1.1 0.4 copy-done.2
  1.6 0.0 copy-done.3
  1.6 0.0 copy-start
  1.6 0.0 copy-start.1
  1.6 0.2 shard_map.56
  1.8 22.2 %all_to_all.15 = bf16[16,16,128]{2,1,0:T(8,128)(2,1)S(1)} all-to-all(bf16[16,16,128]{2,1,0:T(8,128)(2,1)S(1)} %shard_map.56), channel_id=1, replica_groups={{0,32,256,288,64,96,320,352,128,160,384,416,192,224,448,480},{16,48,272..., dimensions={0} | all-to-all | bytes 131072 | tf_op jit(solution)/shard_map/all_to_all | solution.py:188
  24.1 24.8 %all_to_all.16.block_ref = bf16[16,192,128]{2,1,0:T(8,128)(2,1)S(1)} all-to-all(bf16[16,192,128]{2,1,0:T(8,128)(2,1)S(1)} %constant_dynamic-update-slice_fusion), channel_id=1, replica_groups=mesh['row'=32,'col'=16] {'col'}, dimensions={0} | all-to-all | bytes 1572864 | tf_op jit(solution)/shard_map/all_to_all | solution.py:193
  48.9 6.2 %collective-permute-start = (bf16[16,64,128]{2,1,0:T(8,128)(2,1)S(1)}, bf16[16,64,128]{2,1,0:T(8,128)(2,1)S(1)}, u32[]{:S(2)}, u32[]{:S(2)}) collective-permute-start(bf16[16,64,128]{2,1,0:T(8,128)(2,1)S(1)} %slice.4), channel_id=1, source_target_pairs={{0,16},{16,0},{32,48},{48,32},{64,80},{80,64},{96,112},{112,96},{1... | collective-permute-start | bytes 786440 | tf_op jit(solution)/shard_map/ppermute | solution.py:196
  55.2 0.0 copy-done
  55.2 0.0 copy-done.1
  55.2 0.6 shard_map.57
  55.8 0.5 collective-permute-done.other_ref
  56.3 2.0 %shard_map.58 = bf16[4,4,32,128]{3,2,1,0:T(8,128)(2,1)S(1)} custom-call(bf16[16,192,128]{2,1,0:T(8,128)(2,1)S(1)} %all_to_all.16.block_ref, bf16[16,64,128]{2,1,0:T(8,128)(2,1)S(1)} %collective-permute-done.other_ref, bf16[5,640,256]{2,1,0:T(8,128)(2,1)S(1)} %get-tuple-element.11.made_ref, f32[512,512]{1,0:T(8,128)S(1)} %get-tuple-element.12.ahead_ref), custom_call_target="tpu_custom_call" | custom-call | tf_op jit(solution)/shard_map/pallas_call | solution.py:209
  58.3 7.4 %all_to_all.17 = bf16[16,32,128]{2,1,0:T(8,128)(2,1)S(1)} all-to-all(bf16[16,32,128]{2,1,0:T(8,128)(2,1)S(1)} %bitcast.6), channel_id=1, replica_groups={{0,1,8,9},{2,3,10,11},{4,5,12,13},{6,7,14,15},{16,17,24,25},{18,19,26,2..., dimensions={0} | all-to-all | bytes 262144 | tf_op jit(solution)/shard_map/all_to_all | solution.py:220
  65.7 0.7 copy.8
  (3 shorter events, 0.1 us)
Async XLA Ops:
  0.0 0.9 %copy-start.4 = (bf16[16,32,128]{2,1,0:T(8,128)(2,1)S(1)}, bf16[16,32,128]{2,1,0:T(8,128)(2,1)}, u32[]{:S(2)}) copy-start(bf16[16,32,128]{2,1,0:T(8,128)(2,1)} %param.5) | copy-start | bytes 393220
  0.9 0.7 %copy-start.2 = (bf16[128,4]{0,1:T(4,128)(2,1)S(1)}, bf16[128,4]{0,1:T(4,128)(2,1)}, u32[]{:S(2)}) copy-start(bf16[128,4]{0,1:T(4,128)(2,1)} %param.7) | copy-start | bytes 3076
  0.9 0.7 %copy-start.3 = (s32[32]{0:T(128)S(1)}, s32[32]{0:T(128)}, u32[]{:S(2)}) copy-start(s32[32]{0:T(128)} %param.9) | copy-start | bytes 388
  1.6 53.6 %copy-start = (bf16[128,512]{1,0:T(8,128)(2,1)S(1)}, bf16[128,512]{1,0:T(8,128)(2,1)}, u32[]{:S(2)}) copy-start(bf16[128,512]{1,0:T(8,128)(2,1)} %w_proj_ref.1) | copy-start | bytes 393220
  1.6 53.6 %copy-start.1 = (bf16[128,128]{1,0:T(8,128)(2,1)S(1)}, bf16[128,128]{1,0:T(8,128)(2,1)}, u32[]{:S(2)}) copy-start(bf16[128,128]{1,0:T(8,128)(2,1)} %w_out_ref.1) | copy-start | bytes 98308
  48.9 7.4 %collective-permute-start = (bf16[16,64,128]{2,1,0:T(8,128)(2,1)S(1)}, bf16[16,64,128]{2,1,0:T(8,128)(2,1)S(1)}, u32[]{:S(2)}, u32[]{:S(2)}) collective-permute-start(bf16[16,64,128]{2,1,0:T(8,128)(2,1)S(1)} %slice.4), channel_id=1, source_target_pairs={{0,16},{16,0},{32,48},{48,32},{64,80},{80,64},{96,112},{112,96},{1... | collective-permute-start | bytes 786440 | tf_op jit(solution)/shard_map/ppermute | solution.py:196

commit v6 on v5

--- a/solution.py
+++ b/solution.py
@@ -10,6 +10,7 @@
 F32 = jnp.float32
 BF16 = jnp.bfloat16
 VMEM = pl.BlockSpec(memory_space=pltpu.VMEM)
+HBM = pl.BlockSpec(memory_space=pltpu.HBM)
 
 SPLIT = 4
 CORES = 2
@@ -30,16 +31,26 @@
     return (shifted * lax.rsqrt(spread + 1e-05)).astype(BF16)
 
 
-def norm_kernel(pair_ref, send_ref, normed_ref):
+def norm_kernel(
+    rows, cols, pair_hbm, w_bias_hbm, mask_hbm, send_ref, spread_ref, pair_ref, w_bias_ref, mask_ref, read
+):
+    sources = (pair_hbm, w_bias_hbm, mask_hbm)
+    targets = (pair_ref, w_bias_ref, mask_ref)
+    copies = [
+        pltpu.make_async_copy(source, target, read.at[place])
+        for place, (source, target) in enumerate(zip(sources, targets))
+    ]
+    for copy in copies:
+        copy.start()
+    copies[0].wait()
     normed = norm_rows(pair_ref[...].astype(F32))
-    normed_ref[...] = normed
     part = normed.shape[0] // SPLIT
     for member in range(send_ref.shape[0]):
         sub = sub_of(member)
         send_ref[member, 0:part] = normed[sub * part : (sub + 1) * part]
 
-
-def bias_kernel(rows, cols, normed_ref, w_bias_ref, mask_ref, spread_ref):
+    copies[1].wait()
+    copies[2].wait()
     heads, width = w_bias_ref.shape
     head_of_row = lax.broadcasted_iota(jnp.int32, (width, width), 0) // cols
     w_bias = w_bias_ref[...].astype(F32)
@@ -47,7 +58,7 @@
     for head in range(heads):
         wide = jnp.where(head_of_row == head, w_bias[head : head + 1], wide)
     product = lax.dot_general(
-        normed_ref[...], wide.astype(BF16), (((1,), (1,)), ((), ())), preferred_element_type=F32
+        normed, wide.astype(BF16), (((1,), (1,)), ((), ())), preferred_element_type=F32
     )
     column = lax.broadcasted_iota(jnp.int32, product.shape, 0) % cols
     place = lax.broadcasted_iota(jnp.int32, product.shape, 1) % cols
@@ -162,24 +173,24 @@
     depth = queries // CORES
     part = own_rows * cols
 
-    send, normed = pl.pallas_call(
-        norm_kernel,
+    given = (pair.reshape(rows * cols, width), w_bias.T, token_mask[None])
+    given = [pltpu.with_memory_space_constraint(array, pltpu.HBM) for array in given]
+    send, spread = pl.pallas_call(
+        functools.partial(norm_kernel, rows, cols),
         out_shape=(
             jax.ShapeDtypeStruct((col_size, part + depth, width), BF16),
-            jax.ShapeDtypeStruct((rows * cols, width), BF16),
+            jax.ShapeDtypeStruct((half, rows, width), BF16),
         ),
-        in_specs=[VMEM],
+        in_specs=[HBM, HBM, HBM],
         out_specs=(VMEM, VMEM),
+        scratch_shapes=[
+            pltpu.VMEM((rows * cols, width), BF16),
+            pltpu.VMEM((heads, width), BF16),
+            pltpu.VMEM((1, cols), jnp.int32),
+            pltpu.SemaphoreType.DMA((3,)),
+        ],
         compiler_params=pltpu.CompilerParams(vmem_limit_bytes=4 << 20),
-        cost_estimate=pl.CostEstimate(flops=1 << 30, bytes_accessed=16 << 20, transcendentals=0),
-    )(pair.reshape(rows * cols, width))
-    spread = pl.pallas_call(
-        functools.partial(bias_kernel, rows, cols),
-        out_shape=jax.ShapeDtypeStruct((half, rows, width), BF16),
-        in_specs=[VMEM, VMEM, VMEM],
-        out_specs=VMEM,
-        compiler_params=pltpu.CompilerParams(vmem_limit_bytes=4 << 20),
-    )(normed, w_bias.T, token_mask[None])
+    )(*given)
 
     same_core = [
         [CORES * joined(group, sub) + core for group in range(SPLIT) for sub in range(SPLIT)]

time: 66.6 us -> 66.2 us (level)
  local copies, waits for them, and re-layouts: 2.11 us -> 0.76 us
  Pallas kernels: 3.09 us -> 4.06 us
    unnamed x11 -> x5, local copies, waits for them, and re-layouts: 2.01 us -> 0.66 us
    pallas_call x2 -> x1, Pallas kernels: 0.45 us -> 1.42 us  [on_device(): pl.pallas_call(functools.partial(norm_kernel, rows, cols), out_shape=(jax...]
where the time goes in v6:
time: 66.2 us; the launch traced here: 65.9 us
  blocking collectives  54.3 us (82%)
  starting transfers between devices  6.32 us (10%)
  Pallas kernels  4.06 us (6%)
  local copies, waits for them, and re-layouts  0.76 us (1%)
    all_to_all x1, blocking collectives, on_device(): block = lax.all_to_all(send, 'col', 0, 0, tiled=True)  24.7 us
    all_to_all x1, blocking collectives, on_device(): lax.all_to_all(spread, 'row', 0, 0, axis_index_groups=same_core, tiled=True)  22.2 us
    all_to_all x1, blocking collectives, on_device(): lax.all_to_all(answer, 'col', 0, 0, axis_index_groups=near, tiled=True)  7.36 us
    ppermute x1, starting transfers between devices, on_device(): other = lax.ppermute(block[:, part:], 'row', swap)  6.32 us
    pallas_call x1, Pallas kernels, on_device(): pl.pallas_call(functools.partial(attend_kernel, heads, cols), out_shape=j...  2 us
    pallas_call x1, Pallas kernels, on_device(): pl.pallas_call(functools.partial(norm_kernel, rows, cols), out_shape=(jax...  1.42 us
  transfers between devices with their start and end apart: 1, of which 1 were waited for; matrix products, arithmetic and copies ran while one was open for 0% of the time, Pallas kernels for 1%

profile of v6, /device:TPU:1, one launch (start us, length us, event | category | flops | bytes accessed | tf_op | source)
XLA Modules:
  0.0 65.9 jit_solution(18383636543455444377)
XLA Ops:
  0.0 0.0 copy-start.1
  0.0 0.0 copy-start
  0.0 1.4 %shard_map.55 = (bf16[16,192,128]{2,1,0:T(8,128)(2,1)S(1)}, bf16[16,16,128]{2,1,0:T(8,128)(2,1)S(1)}) custom-call(bf16[512,128]{1,0:T(8,128)(2,1)} %bitcast.9, bf16[4,128]{1,0:T(4,128)(2,1)} %bitcast.10, s32[1,32]{1,0:T(1,128)} %bitcast.11), custom_call_target="tpu_custom_call" | custom-call | tf_op jit(solution)/shard_map/pallas_call | solution.py:178
  1.4 22.2 %all_to_all.15 = bf16[16,16,128]{2,1,0:T(8,128)(2,1)S(1)} all-to-all(bf16[16,16,128]{2,1,0:T(8,128)(2,1)S(1)} %get-tuple-element.10), channel_id=1, replica_groups={{0,32,256,288,64,96,320,352,128,160,384,416,192,224,448,480},{16,48,272..., dimensions={0} | all-to-all | bytes 131072 | tf_op jit(solution)/shard_map/all_to_all | solution.py:199
  23.7 24.7 %all_to_all.16.block_ref = bf16[16,192,128]{2,1,0:T(8,128)(2,1)S(1)} all-to-all(bf16[16,192,128]{2,1,0:T(8,128)(2,1)S(1)} %constant_dynamic-update-slice_fusion), channel_id=1, replica_groups=mesh['row'=32,'col'=16] {'col'}, dimensions={0} | all-to-all | bytes 1572864 | tf_op jit(solution)/shard_map/all_to_all | solution.py:204
  48.4 6.3 %collective-permute-start = (bf16[16,64,128]{2,1,0:T(8,128)(2,1)S(1)}, bf16[16,64,128]{2,1,0:T(8,128)(2,1)S(1)}, u32[]{:S(2)}, u32[]{:S(2)}) collective-permute-start(bf16[16,64,128]{2,1,0:T(8,128)(2,1)S(1)} %slice.4), channel_id=1, source_target_pairs={{0,16},{16,0},{32,48},{48,32},{64,80},{80,64},{96,112},{112,96},{1... | collective-permute-start | bytes 786440 | tf_op jit(solution)/shard_map/ppermute | solution.py:207
  54.8 0.0 copy-done.1
  54.8 0.0 copy-done
  54.8 0.6 shard_map.56
  55.4 0.5 collective-permute-done.other_ref
  55.9 2.0 %shard_map.57 = bf16[4,4,32,128]{3,2,1,0:T(8,128)(2,1)S(1)} custom-call(bf16[16,192,128]{2,1,0:T(8,128)(2,1)S(1)} %all_to_all.16.block_ref, bf16[16,64,128]{2,1,0:T(8,128)(2,1)S(1)} %collective-permute-done.other_ref, bf16[5,640,256]{2,1,0:T(8,128)(2,1)S(1)} %get-tuple-element.11.made_ref, f32[512,512]{1,0:T(8,128)S(1)} %get-tuple-element.12.ahead_ref), custom_call_target="tpu_custom_call" | custom-call | tf_op jit(solution)/shard_map/pallas_call | solution.py:220
  57.9 7.4 %all_to_all.17 = bf16[16,32,128]{2,1,0:T(8,128)(2,1)S(1)} all-to-all(bf16[16,32,128]{2,1,0:T(8,128)(2,1)S(1)} %bitcast.6), channel_id=1, replica_groups={{0,1,8,9},{2,3,10,11},{4,5,12,13},{6,7,14,15},{16,17,24,25},{18,19,26,2..., dimensions={0} | all-to-all | bytes 262144 | tf_op jit(solution)/shard_map/all_to_all | solution.py:231
  65.3 0.7 copy.8
  (3 shorter events, 0.1 us)
Async XLA Ops:
  0.0 54.8 %copy-start.1 = (bf16[128,128]{1,0:T(8,128)(2,1)S(1)}, bf16[128,128]{1,0:T(8,128)(2,1)}, u32[]{:S(2)}) copy-start(bf16[128,128]{1,0:T(8,128)(2,1)} %w_out_ref.1) | copy-start | bytes 98308
  0.0 54.8 %copy-start = (bf16[128,512]{1,0:T(8,128)(2,1)S(1)}, bf16[128,512]{1,0:T(8,128)(2,1)}, u32[]{:S(2)}) copy-start(bf16[128,512]{1,0:T(8,128)(2,1)} %w_proj_ref.1) | copy-start | bytes 393220
  48.4 7.5 %collective-permute-start = (bf16[16,64,128]{2,1,0:T(8,128)(2,1)S(1)}, bf16[16,64,128]{2,1,0:T(8,128)(2,1)S(1)}, u32[]{:S(2)}, u32[]{:S(2)}) collective-permute-start(bf16[16,64,128]{2,1,0:T(8,128)(2,1)S(1)} %slice.4), channel_id=1, source_target_pairs={{0,16},{16,0},{32,48},{48,32},{64,80},{80,64},{96,112},{112,96},{1... | collective-permute-start | bytes 786440 | tf_op jit(solution)/shard_map/ppermute | solution.py:207

commit v7 on v6

--- a/solution.py
+++ b/solution.py
@@ -14,6 +14,7 @@
 
 SPLIT = 4
 CORES = 2
+PAIR = 4
 
 
 def joined(group, sub):
@@ -71,24 +72,12 @@
         spread_ref[member] = bias
 
 
-def products(heads, keys_count, made_ref, row):
-    width = made_ref.shape[2] // 2
-    lane_head = lax.broadcasted_iota(jnp.int32, (1, width), 1) // (width // heads)
-    query = made_ref[row, keys_count:, :width].astype(F32)
-    wide = [jnp.where(lane_head == head, query, 0.0).astype(BF16) for head in range(heads)]
-    return lax.dot_general(
-        jnp.concatenate(wide, axis=0),
-        made_ref[row, :keys_count, :width],
-        (((1,), (1,)), ((), ())),
-        preferred_element_type=F32,
-    )
-
-
-def project_kernel(heads, cols, own_rows, block_ref, w_proj_ref, w_out_ref, made_ref, ahead_ref):
+def project(heads, cols, own_rows, block_ref, w_proj_ref, w_out_ref, made_ref):
     members, _, width = block_ref.shape
     head_size = width // heads
     keys_count = members * cols
     queries = SPLIT * cols
+    tall = cols // CORES
     first = lax.axis_index("col") // 2 % SPLIT * 2
     for row in range(own_rows):
         entries = block_ref[:, row * cols : (row + 1) * cols].reshape(keys_count, width)
@@ -96,7 +85,8 @@
             entries, w_proj_ref[:, width : 3 * width], preferred_element_type=F32
         ).astype(BF16)
         asking = [
-            block_ref[pl.ds(first + start, 2), row * cols : (row + 1) * cols]
+            block_ref[pl.ds(first + start, 2), row * cols + core * tall : row * cols + (core + 1) * tall]
+            for core in range(CORES)
             for start in (0, 2 * SPLIT)
         ]
         asking = jnp.concatenate(asking, axis=0).reshape(queries, width)
@@ -105,62 +95,83 @@
         gates = jnp.dot(asking, w_proj_ref[:, 3 * width :], preferred_element_type=F32)
         made_ref[row, keys_count:, width:] = gates.astype(BF16)
     made_ref[own_rows, :width, :width] = w_out_ref[...]
-    ahead_ref[...] = products(heads, keys_count, made_ref, 0)
-
-
-def attend_kernel(heads, cols, block_ref, other_ref, made_ref, ahead_ref, out_ref, bias_ref):
-    members, depth, width = other_ref.shape
+
+
+def attend(heads, cols, core, source_ref, made_ref, out_ref, bias_ref):
+    members, chunk, width = source_ref.shape
+    depth = bias_ref.shape[1]
     own_rows = made_ref.shape[0] - 1
-    queries = SPLIT * cols
     keys_count = members * cols
     group = width // cols
-    part = block_ref.shape[1] - depth
-    parity = lax.axis_index("row") % CORES
-
+    tall = depth // SPLIT
     lane_head = lax.broadcasted_iota(jnp.int32, (1, width), 1) // (width // heads)
-
+    asking = pl.ds(pl.multiple_of(keys_count + core * depth, depth), depth)
+
+    def products(row):
+        query = made_ref[row, asking, :width].astype(F32)
+        wide = [jnp.where(lane_head == head, query, 0.0).astype(BF16) for head in range(heads)]
+        return lax.dot_general(
+            jnp.concatenate(wide, axis=0),
+            made_ref[row, :keys_count, :width],
+            (((1,), (1,)), ((), ())),
+            preferred_element_type=F32,
+        )
+
+    ahead = products(0)
     segment = lax.broadcasted_iota(jnp.int32, (1, width), 1) // cols
     for turn in range(members // group):
-        for source in range(CORES):
-            turned = []
-            for piece in range(group):
-                member = turn * group + piece
-                value = other_ref[member] if source else block_ref[member, part:]
-                value = value.astype(F32)
-                turned.append([value] + [pltpu.roll(value, cols * d, 1) for d in range(1, group)])
-            core = 1 - parity if source else parity
-            for head in range(heads):
-                value = turned[0][-head % group]
-                for piece in range(1, group):
-                    value = jnp.where(segment == piece, turned[piece][(piece - head) % group], value)
-                value = value.reshape(SPLIT, depth // SPLIT, width)
-                bias_ref[head, :, core, :, turn * width : (turn + 1) * width] = value
+        turned = []
+        for piece in range(group):
+            value = source_ref[turn * group + piece, chunk - depth :].astype(F32)
+            turned.append([value] + [pltpu.roll(value, cols * d, 1) for d in range(1, group)])
+        for head in range(heads):
+            value = turned[0][-head % group]
+            for piece in range(1, group):
+                value = jnp.where(segment == piece, turned[piece][(piece - head) % group], value)
+            bias_ref[head, :, turn * width : (turn + 1) * width] = value
 
     w_out = made_ref[own_rows, :width, :width]
     ones = jnp.ones((keys_count, width), BF16)
     gated = []
     for row in range(own_rows):
-        scores = ahead_ref if row == 0 else ahead
+        scores = ahead
         if row + 1 < own_rows:
-            ahead = products(heads, keys_count, made_ref, row + 1)
+            ahead = products(row + 1)
+        values = jnp.concatenate([made_ref[row, :keys_count, width:], ones], axis=1)
         weights = []
         for head in range(heads):
-            value = scores[head * queries : (head + 1) * queries]
-            value = value + bias_ref[head].reshape(queries, keys_count)
+            value = scores[head * depth : (head + 1) * depth] + bias_ref[head]
             top = jnp.max(value, axis=-1, keepdims=True)
             weights.append(jnp.exp(value - top).astype(BF16))
-        values = jnp.concatenate([made_ref[row, :keys_count, width:], ones], axis=1)
-        above = jnp.zeros((queries, width), F32)
-        below = jnp.zeros((queries, width), F32)
-        for head in range(heads):
-            sums = jnp.dot(weights[head], values, preferred_element_type=F32)
-            above = jnp.where(lane_head == head, sums[:, :width], above)
-            below = jnp.where(lane_head == head, sums[:, width:], below)
-        gates = made_ref[row, keys_count:, width:].astype(F32)
+        above = jnp.zeros((depth, width), F32)
+        below = jnp.zeros((depth, width), F32)
+        for pair in range(0, heads, PAIR):
+            both = jnp.concatenate(weights[pair : pair + PAIR], axis=0)
+            sums = jnp.dot(both, values, preferred_element_type=F32)
+            for head in range(pair, pair + PAIR):
+                chosen = slice((head - pair) * depth, (head - pair + 1) * depth)
+                above = jnp.where(lane_head == head, sums[chosen, :width], above)
+                below = jnp.where(lane_head == head, sums[chosen, width:], below)
+        gates = made_ref[row, asking, width:].astype(F32)
         gated.append((above / below * jax.nn.sigmoid(gates)).astype(BF16))
     result = jnp.dot(jnp.concatenate(gated, axis=0), w_out, preferred_element_type=F32).astype(BF16)
+    place = pl.ds(pl.multiple_of(core * tall, tall), tall)
     for row in range(own_rows):
-        out_ref[:, row] = result[row * queries : (row + 1) * queries].reshape(SPLIT, cols, width)
+        for sub in range(SPLIT):
+            start = row * depth + sub * tall
+            out_ref[sub, row, place] = result[start : start + tall]
+
+
+def own_kernel(heads, cols, own_rows, block_ref, w_proj_ref, w_out_ref, made_ref, out_ref, bias_ref):
+    project(heads, cols, own_rows, block_ref, w_proj_ref, w_out_ref, made_ref)
+    core = lax.axis_index("row") % CORES
+    attend(heads, cols, core, block_ref, made_ref, out_ref, bias_ref)
+
+
+def other_kernel(heads, cols, other_ref, made_ref, half_ref, out_ref, bias_ref):
+    del half_ref
+    core = 1 - lax.axis_index("row") % CORES
+    attend(heads, cols, core, other_ref, made_ref, out_ref, bias_ref)
 
 
 def on_device(pair, w_proj, w_bias, w_out, token_mask, *, row_size, col_size):
@@ -206,25 +217,27 @@
     swap = [(r, r ^ 1) for r in range(row_size)]
     other = lax.ppermute(block[:, part:], "row", swap)
 
-    made, ahead = pl.pallas_call(
-        functools.partial(project_kernel, heads, cols, own_rows),
-        out_shape=(
-            jax.ShapeDtypeStruct((own_rows + 1, keys_count + queries, 2 * width), BF16),
-            jax.ShapeDtypeStruct((heads * queries, keys_count), F32),
-        ),
+    made_shape = jax.ShapeDtypeStruct((own_rows + 1, keys_count + queries, 2 * width), BF16)
+    answer_shape = jax.ShapeDtypeStruct((SPLIT, own_rows, cols, width), BF16)
+    scratch = [pltpu.VMEM((heads, depth, keys_count), F32)]
+    params = pltpu.CompilerParams(vmem_limit_bytes=12 << 20)
+    made, answer = pl.pallas_call(
+        functools.partial(own_kernel, heads, cols, own_rows),
+        out_shape=(made_shape, answer_shape),
         in_specs=[VMEM, VMEM, VMEM],
         out_specs=(VMEM, VMEM),
-        compiler_params=pltpu.CompilerParams(vmem_limit_bytes=12 << 20),
+        scratch_shapes=scratch,
+        compiler_params=params,
     )(block, w_proj, w_out)
-
     answer = pl.pallas_call(
-        functools.partial(attend_kernel, heads, cols),
-        out_shape=jax.ShapeDtypeStruct((SPLIT, own_rows, cols, width), BF16),
-        in_specs=[VMEM, VMEM, VMEM, VMEM],
+        functools.partial(other_kernel, heads, cols),
+        out_shape=answer_shape,
+        in_specs=[VMEM, VMEM, VMEM],
         out_specs=VMEM,
-        scratch_shapes=[pltpu.VMEM((heads, SPLIT, CORES, depth // SPLIT, keys_count), F32)],
-        compiler_params=pltpu.CompilerParams(vmem_limit_bytes=12 << 20),
-    )(block, other, made, ahead)
+        scratch_shapes=scratch,
+        input_output_aliases={2: 0},
+        compiler_params=params,
+    )(other, made, answer)
 
     near = [[joined(group, sub) for sub in range(SPLIT)] for group in range(SPLIT)]
     answer = answer.reshape(rows, cols, width)

time: 66.2 us -> 65.9 us (level)
  transfers between devices with their start and end apart: 1 -> 1, of which waited for: 1 -> 0; matrix products, arithmetic and copies ran while one was open for 0% -> 0% of each run, Pallas kernels for 1% -> 2%
where the time goes in v7:
time: 65.9 us; the launch traced here: 65.7 us
  blocking collectives  54.4 us (83%)
  starting transfers between devices  6.32 us (10%)
  Pallas kernels  4.17 us (6%)
  local copies, waits for them, and re-layouts  0.76 us (1%)
    all_to_all x1, blocking collectives, on_device(): block = lax.all_to_all(send, 'col', 0, 0, tiled=True)  24.7 us
    all_to_all x1, blocking collectives, on_device(): lax.all_to_all(spread, 'row', 0, 0, axis_index_groups=same_core, tiled=True)  22.2 us
    all_to_all x1, blocking collectives, on_device(): lax.all_to_all(answer, 'col', 0, 0, axis_index_groups=near, tiled=True)  7.46 us
    ppermute x1, starting transfers between devices, on_device(): other = lax.ppermute(block[:, part:], 'row', swap)  6.32 us
    pallas_call x1, Pallas kernels, on_device(): pl.pallas_call(functools.partial(own_kernel, heads, cols, own_rows), out_...  1.47 us
    pallas_call x1, Pallas kernels, on_device(): pl.pallas_call(functools.partial(norm_kernel, rows, cols), out_shape=(jax...  1.42 us
  transfers between devices with their start and end apart: 1, of which 0 were waited for; matrix products, arithmetic and copies ran while one was open for 0% of the time, Pallas kernels for 2%

profile of v7, /device:TPU:1, one launch (start us, length us, event | category | flops | bytes accessed | tf_op | source)
XLA Modules:
  0.0 65.7 jit_solution(12840051425399019539)
XLA Ops:
  0.0 0.0 copy-start
  0.0 0.0 copy-start.1
  0.0 1.4 %shard_map.55 = (bf16[16,192,128]{2,1,0:T(8,128)(2,1)S(1)}, bf16[16,16,128]{2,1,0:T(8,128)(2,1)S(1)}) custom-call(bf16[512,128]{1,0:T(8,128)(2,1)} %bitcast.9, bf16[4,128]{1,0:T(4,128)(2,1)} %bitcast.10, s32[1,32]{1,0:T(1,128)} %bitcast.11), custom_call_target="tpu_custom_call" | custom-call | tf_op jit(solution)/shard_map/pallas_call | solution.py:189
  1.4 22.2 %all_to_all.15 = bf16[16,16,128]{2,1,0:T(8,128)(2,1)S(1)} all-to-all(bf16[16,16,128]{2,1,0:T(8,128)(2,1)S(1)} %get-tuple-element.10), channel_id=1, replica_groups={{0,32,256,288,64,96,320,352,128,160,384,416,192,224,448,480},{16,48,272..., dimensions={0} | all-to-all | bytes 131072 | tf_op jit(solution)/shard_map/all_to_all | solution.py:210
  23.7 24.7 %all_to_all.16.block_ref = bf16[16,192,128]{2,1,0:T(8,128)(2,1)S(1)} all-to-all(bf16[16,192,128]{2,1,0:T(8,128)(2,1)S(1)} %constant_dynamic-update-slice_fusion), channel_id=1, replica_groups=mesh['row'=32,'col'=16] {'col'}, dimensions={0} | all-to-all | bytes 1572864 | tf_op jit(solution)/shard_map/all_to_all | solution.py:215
  48.4 6.3 %collective-permute-start = (bf16[16,64,128]{2,1,0:T(8,128)(2,1)S(1)}, bf16[16,64,128]{2,1,0:T(8,128)(2,1)S(1)}, u32[]{:S(2)}, u32[]{:S(2)}) collective-permute-start(bf16[16,64,128]{2,1,0:T(8,128)(2,1)S(1)} %slice.4), channel_id=1, source_target_pairs={{0,16},{16,0},{32,48},{48,32},{64,80},{80,64},{96,112},{112,96},{1... | collective-permute-start | bytes 786440 | tf_op jit(solution)/shard_map/ppermute | solution.py:218
  54.8 0.0 copy-done
  54.8 0.0 copy-done.1
  54.8 1.5 %shard_map.56 = (bf16[5,640,256]{2,1,0:T(8,128)(2,1)S(1)}, bf16[4,4,32,128]{3,2,1,0:T(8,128)(2,1)S(1)}) custom-call(bf16[16,192,128]{2,1,0:T(8,128)(2,1)S(1)} %all_to_all.16.block_ref, bf16[128,512]{1,0:T(8,128)(2,1)S(1)} %copy-done, bf16[128,128]{1,0:T(8,128)(2,1)S(1)} %copy-done.1), custom_call_target="tpu_custom_call" | custom-call | tf_op jit(solution)/shard_map/pallas_call | solution.py:224
  56.3 0.0 collective-permute-done.other_ref
  56.3 1.3 %shard_map.57 = bf16[4,4,32,128]{3,2,1,0:T(8,128)(2,1)S(1)} custom-call(bf16[16,64,128]{2,1,0:T(8,128)(2,1)S(1)} %collective-permute-done.other_ref, bf16[5,640,256]{2,1,0:T(8,128)(2,1)S(1)} %get-tuple-element.11.made_ref, bf16[4,4,32,128]{3,2,1,0:T(8,128)(2,1)S(1)} %get-tuple-element.12.half_ref), custom_call_target="tpu_custom_call", output_to_operand_aliasing={{}: (2, {})} | custom-call | tf_op jit(solution)/shard_map/pallas_call | solution.py:232
  57.6 7.5 %all_to_all.17 = bf16[16,32,128]{2,1,0:T(8,128)(2,1)S(1)} all-to-all(bf16[16,32,128]{2,1,0:T(8,128)(2,1)S(1)} %bitcast.6), channel_id=1, replica_groups={{0,1,8,9},{2,3,10,11},{4,5,12,13},{6,7,14,15},{16,17,24,25},{18,19,26,2..., dimensions={0} | all-to-all | bytes 262144 | tf_op jit(solution)/shard_map/all_to_all | solution.py:244
  65.0 0.7 copy.10
  (3 shorter events, 0.1 us)
Async XLA Ops:
  0.0 54.8 %copy-start = (bf16[128,512]{1,0:T(8,128)(2,1)S(1)}, bf16[128,512]{1,0:T(8,128)(2,1)}, u32[]{:S(2)}) copy-start(bf16[128,512]{1,0:T(8,128)(2,1)} %w_proj_ref.1) | copy-start | bytes 393220
  0.0 54.8 %copy-start.1 = (bf16[128,128]{1,0:T(8,128)(2,1)S(1)}, bf16[128,128]{1,0:T(8,128)(2,1)}, u32[]{:S(2)}) copy-start(bf16[128,128]{1,0:T(8,128)(2,1)} %w_out_ref.1) | copy-start | bytes 98308
  48.4 7.8 %collective-permute-start = (bf16[16,64,128]{2,1,0:T(8,128)(2,1)S(1)}, bf16[16,64,128]{2,1,0:T(8,128)(2,1)S(1)}, u32[]{:S(2)}, u32[]{:S(2)}) collective-permute-start(bf16[16,64,128]{2,1,0:T(8,128)(2,1)S(1)} %slice.4), channel_id=1, source_target_pairs={{0,16},{16,0},{32,48},{48,32},{64,80},{80,64},{96,112},{112,96},{1... | collective-permute-start | bytes 786440 | tf_op jit(solution)/shard_map/ppermute | solution.py:218

commit v8 on v7

--- a/solution.py
+++ b/solution.py
@@ -33,7 +33,7 @@
 
 
 def norm_kernel(
-    rows, cols, pair_hbm, w_bias_hbm, mask_hbm, send_ref, spread_ref, pair_ref, w_bias_ref, mask_ref, read
+    rows, cols, pair_hbm, w_bias_hbm, mask_hbm, send_ref, spread_ref, pair_ref, w_bias_ref, mask_ref, normed_ref, read
 ):
     sources = (pair_hbm, w_bias_hbm, mask_hbm)
     targets = (pair_ref, w_bias_ref, mask_ref)
@@ -45,10 +45,15 @@
         copy.start()
     copies[0].wait()
     normed = norm_rows(pair_ref[...].astype(F32))
+    normed_ref[...] = normed
     part = normed.shape[0] // SPLIT
-    for member in range(send_ref.shape[0]):
-        sub = sub_of(member)
-        send_ref[member, 0:part] = normed[sub * part : (sub + 1) * part]
+    flip = lax.axis_index("row") % CORES
+    for sub in range(SPLIT):
+        start = pl.multiple_of(((sub // 2 + flip) % 2 * 2 + sub % 2) * part, part)
+        piece = normed_ref[pl.ds(start, part)]
+        for member in range(send_ref.shape[0]):
+            if sub_of(member) == sub:
+                send_ref[member, 0:part] = piece
 
     copies[1].wait()
     copies[2].wait()
@@ -79,15 +84,16 @@
     queries = SPLIT * cols
     tall = cols // CORES
     first = lax.axis_index("col") // 2 % SPLIT * 2
+    flip = lax.axis_index("row") % CORES
     for row in range(own_rows):
         entries = block_ref[:, row * cols : (row + 1) * cols].reshape(keys_count, width)
         made_ref[row, :keys_count] = jnp.dot(
             entries, w_proj_ref[:, width : 3 * width], preferred_element_type=F32
         ).astype(BF16)
         asking = [
-            block_ref[pl.ds(first + start, 2), row * cols + core * tall : row * cols + (core + 1) * tall]
+            block_ref[pl.ds(first + (high + flip) % 2 * (2 * SPLIT), 2), row * cols + core * tall : row * cols + (core + 1) * tall]
             for core in range(CORES)
-            for start in (0, 2 * SPLIT)
+            for high in range(2)
         ]
         asking = jnp.concatenate(asking, axis=0).reshape(queries, width)
         query = jnp.dot(asking, w_proj_ref[:, :width], preferred_element_type=F32)
@@ -97,7 +103,7 @@
     made_ref[own_rows, :width, :width] = w_out_ref[...]
 
 
-def attend(heads, cols, core, source_ref, made_ref, out_ref, bias_ref):
+def attend(heads, cols, core, shift, source_ref, made_ref, out_ref, bias_ref):
     members, chunk, width = source_ref.shape
     depth = bias_ref.shape[1]
     own_rows = made_ref.shape[0] - 1
@@ -122,7 +128,8 @@
     for turn in range(members // group):
         turned = []
         for piece in range(group):
-            value = source_ref[turn * group + piece, chunk - depth :].astype(F32)
+            member = (turn * group + piece + shift) % members
+            value = source_ref[member, chunk - depth :].astype(F32)
             turned.append([value] + [pltpu.roll(value, cols * d, 1) for d in range(1, group)])
         for head in range(heads):
             value = turned[0][-head % group]
@@ -165,13 +172,13 @@
 def own_kernel(heads, cols, own_rows, block_ref, w_proj_ref, w_out_ref, made_ref, out_ref, bias_ref):
     project(heads, cols, own_rows, block_ref, w_proj_ref, w_out_ref, made_ref)
     core = lax.axis_index("row") % CORES
-    attend(heads, cols, core, block_ref, made_ref, out_ref, bias_ref)
+    attend(heads, cols, core, 0, block_ref, made_ref, out_ref, bias_ref)
 
 
 def other_kernel(heads, cols, other_ref, made_ref, half_ref, out_ref, bias_ref):
     del half_ref
     core = 1 - lax.axis_index("row") % CORES
-    attend(heads, cols, core, other_ref, made_ref, out_ref, bias_ref)
+    attend(heads, cols, core, other_ref.shape[0] // 2, other_ref, made_ref, out_ref, bias_ref)
 
 
 def on_device(pair, w_proj, w_bias, w_out, token_mask, *, row_size, col_size):
@@ -198,6 +205,7 @@
             pltpu.VMEM((rows * cols, width), BF16),
             pltpu.VMEM((heads, width), BF16),
             pltpu.VMEM((1, cols), jnp.int32),
+            pltpu.VMEM((rows * cols, width), BF16),
             pltpu.SemaphoreType.DMA((3,)),
         ],
         compiler_params=pltpu.CompilerParams(vmem_limit_bytes=4 << 20),
@@ -212,7 +220,11 @@
     bias = bias.reshape(1, SPLIT, 1, depth, width)
     bias = jnp.broadcast_to(bias, (2, SPLIT, 2, depth, width)).reshape(col_size, depth, width)
     send = lax.dynamic_update_slice(send, bias, (0, part, 0))
-    block = lax.all_to_all(send, "col", 0, 0, tiled=True)
+    orders = [
+        [row * col_size + (col + row % CORES * (col_size // 2)) % col_size for col in range(col_size)]
+        for row in range(row_size)
+    ]
+    block = lax.all_to_all(send, ("row", "col"), 0, 0, axis_index_groups=orders, tiled=True)
 
     swap = [(r, r ^ 1) for r in range(row_size)]
     other = lax.ppermute(block[:, part:], "row", swap)

time: 65.9 us -> 66.1 us (level)
    all_to_all x1, blocking collectives: 7.46 us -> 6.75 us  [on_device(): lax.all_to_all(answer, 'col', 0, 0, axis_index_groups=near, tiled=True)]
where the time goes in v8:
time: 66.1 us; the launch traced here: 65.9 us
  blocking collectives  54.2 us (82%)
  starting transfers between devices  6.66 us (10%)
  Pallas kernels  4.21 us (6%)
  local copies, waits for them, and re-layouts  0.76 us (1%)
    all_to_all x1, blocking collectives, on_device(): lax.all_to_all(send, ('row', 'col'), 0, 0, axis_index_groups=orders, tile...  25.3 us
    all_to_all x1, blocking collectives, on_device(): lax.all_to_all(spread, 'row', 0, 0, axis_index_groups=same_core, tiled=True)  22.2 us
    all_to_all x1, blocking collectives, on_device(): lax.all_to_all(answer, 'col', 0, 0, axis_index_groups=near, tiled=True)  6.75 us
    ppermute x1, starting transfers between devices, on_device(): other = lax.ppermute(block[:, part:], 'row', swap)  6.66 us
    pallas_call x1, Pallas kernels, on_device(): pl.pallas_call(functools.partial(norm_kernel, rows, cols), out_shape=(jax...  1.5 us
    pallas_call x1, Pallas kernels, on_device(): pl.pallas_call(functools.partial(own_kernel, heads, cols, own_rows), out_...  1.43 us
  transfers between devices with their start and end apart: 1, of which 0 were waited for; matrix products, arithmetic and copies ran while one was open for 0% of the time, Pallas kernels for 2%

profile of v8, /device:TPU:1, one launch (start us, length us, event | category | flops | bytes accessed | tf_op | source)
XLA Modules:
  0.0 65.9 jit_solution(5850549291110493105)
XLA Ops:
  0.0 0.0 copy-start
  0.0 0.0 copy-start.1
  0.0 1.5 %shard_map.55 = (bf16[16,192,128]{2,1,0:T(8,128)(2,1)S(1)}, bf16[16,16,128]{2,1,0:T(8,128)(2,1)S(1)}) custom-call(bf16[512,128]{1,0:T(8,128)(2,1)} %bitcast.9, bf16[4,128]{1,0:T(4,128)(2,1)} %bitcast.10, s32[1,32]{1,0:T(1,128)} %bitcast.11), custom_call_target="tpu_custom_call" | custom-call | tf_op jit(solution)/shard_map/pallas_call | solution.py:196
  1.5 22.2 %all_to_all.15 = bf16[16,16,128]{2,1,0:T(8,128)(2,1)S(1)} all-to-all(bf16[16,16,128]{2,1,0:T(8,128)(2,1)S(1)} %get-tuple-element.10), channel_id=1, replica_groups={{0,32,256,288,64,96,320,352,128,160,384,416,192,224,448,480},{16,48,272..., dimensions={0} | all-to-all | bytes 131072 | tf_op jit(solution)/shard_map/all_to_all | solution.py:218
  23.8 25.3 %all_to_all.16.block_ref = bf16[16,192,128]{2,1,0:T(8,128)(2,1)S(1)} all-to-all(bf16[16,192,128]{2,1,0:T(8,128)(2,1)S(1)} %constant_dynamic-update-slice_fusion), channel_id=1, replica_groups={{0,1,2,3,4,5,6,7,8,9,10,11,12,13,14,15},{24,25,26,27,28,29,30,31,16,17,..., dimensions={0} | all-to-all | bytes 1572864 | tf_op jit(solution)/shard_map/all_to_all | solution.py:227
  49.0 6.7 %collective-permute-start = (bf16[16,64,128]{2,1,0:T(8,128)(2,1)S(1)}, bf16[16,64,128]{2,1,0:T(8,128)(2,1)S(1)}, u32[]{:S(2)}, u32[]{:S(2)}) collective-permute-start(bf16[16,64,128]{2,1,0:T(8,128)(2,1)S(1)} %slice.4), channel_id=1, source_target_pairs={{0,16},{16,0},{32,48},{48,32},{64,80},{80,64},{96,112},{112,96},{1... | collective-permute-start | bytes 786440 | tf_op jit(solution)/shard_map/ppermute | solution.py:230
  55.7 0.0 copy-done
  55.7 0.0 copy-done.1
  55.7 1.4 %shard_map.56 = (bf16[5,640,256]{2,1,0:T(8,128)(2,1)S(1)}, bf16[4,4,32,128]{3,2,1,0:T(8,128)(2,1)S(1)}) custom-call(bf16[16,192,128]{2,1,0:T(8,128)(2,1)S(1)} %all_to_all.16.block_ref, bf16[128,512]{1,0:T(8,128)(2,1)S(1)} %copy-done, bf16[128,128]{1,0:T(8,128)(2,1)S(1)} %copy-done.1), custom_call_target="tpu_custom_call" | custom-call | tf_op jit(solution)/shard_map/pallas_call | solution.py:236
  57.2 0.0 collective-permute-done.other_ref
  57.2 1.3 %shard_map.57 = bf16[4,4,32,128]{3,2,1,0:T(8,128)(2,1)S(1)} custom-call(bf16[16,64,128]{2,1,0:T(8,128)(2,1)S(1)} %collective-permute-done.other_ref, bf16[5,640,256]{2,1,0:T(8,128)(2,1)S(1)} %get-tuple-element.11.made_ref, bf16[4,4,32,128]{3,2,1,0:T(8,128)(2,1)S(1)} %get-tuple-element.12.half_ref), custom_call_target="tpu_custom_call", output_to_operand_aliasing={{}: (2, {})} | custom-call | tf_op jit(solution)/shard_map/pallas_call | solution.py:244
  58.5 6.8 %all_to_all.17 = bf16[16,32,128]{2,1,0:T(8,128)(2,1)S(1)} all-to-all(bf16[16,32,128]{2,1,0:T(8,128)(2,1)S(1)} %bitcast.6), channel_id=1, replica_groups={{0,1,8,9},{2,3,10,11},{4,5,12,13},{6,7,14,15},{16,17,24,25},{18,19,26,2..., dimensions={0} | all-to-all | bytes 262144 | tf_op jit(solution)/shard_map/all_to_all | solution.py:256
  65.2 0.7 copy.10
  (3 shorter events, 0.1 us)
Async XLA Ops:
  0.0 55.7 %copy-start = (bf16[128,512]{1,0:T(8,128)(2,1)S(1)}, bf16[128,512]{1,0:T(8,128)(2,1)}, u32[]{:S(2)}) copy-start(bf16[128,512]{1,0:T(8,128)(2,1)} %w_proj_ref.1) | copy-start | bytes 393220
  0.0 55.7 %copy-start.1 = (bf16[128,128]{1,0:T(8,128)(2,1)S(1)}, bf16[128,128]{1,0:T(8,128)(2,1)}, u32[]{:S(2)}) copy-start(bf16[128,128]{1,0:T(8,128)(2,1)} %w_out_ref.1) | copy-start | bytes 98308
  49.0 8.1 %collective-permute-start = (bf16[16,64,128]{2,1,0:T(8,128)(2,1)S(1)}, bf16[16,64,128]{2,1,0:T(8,128)(2,1)S(1)}, u32[]{:S(2)}, u32[]{:S(2)}) collective-permute-start(bf16[16,64,128]{2,1,0:T(8,128)(2,1)S(1)} %slice.4), channel_id=1, source_target_pairs={{0,16},{16,0},{32,48},{48,32},{64,80},{80,64},{96,112},{112,96},{1... | collective-permute-start | bytes 786440 | tf_op jit(solution)/shard_map/ppermute | solution.py:230

commit v9 on v7

--- a/solution.py
+++ b/solution.py
@@ -72,7 +72,7 @@
         spread_ref[member] = bias
 
 
-def project(heads, cols, own_rows, block_ref, w_proj_ref, w_out_ref, made_ref):
+def project(heads, cols, own_rows, block_ref, w_proj_ref, made_ref):
     members, _, width = block_ref.shape
     head_size = width // heads
     keys_count = members * cols
@@ -94,13 +94,12 @@
         made_ref[row, keys_count:, :width] = (query * head_size ** (-0.5)).astype(BF16)
         gates = jnp.dot(asking, w_proj_ref[:, 3 * width :], preferred_element_type=F32)
         made_ref[row, keys_count:, width:] = gates.astype(BF16)
-    made_ref[own_rows, :width, :width] = w_out_ref[...]
 
 
 def attend(heads, cols, core, source_ref, made_ref, out_ref, bias_ref):
     members, chunk, width = source_ref.shape
     depth = bias_ref.shape[1]
-    own_rows = made_ref.shape[0] - 1
+    own_rows = made_ref.shape[0]
     keys_count = members * cols
     group = width // cols
     tall = depth // SPLIT
@@ -130,7 +129,6 @@
                 value = jnp.where(segment == piece, turned[piece][(piece - head) % group], value)
             bias_ref[head, :, turn * width : (turn + 1) * width] = value
 
-    w_out = made_ref[own_rows, :width, :width]
     ones = jnp.ones((keys_count, width), BF16)
     gated = []
     for row in range(own_rows):
@@ -154,16 +152,14 @@
                 below = jnp.where(lane_head == head, sums[chosen, width:], below)
         gates = made_ref[row, asking, width:].astype(F32)
         gated.append((above / below * jax.nn.sigmoid(gates)).astype(BF16))
-    result = jnp.dot(jnp.concatenate(gated, axis=0), w_out, preferred_element_type=F32).astype(BF16)
     place = pl.ds(pl.multiple_of(core * tall, tall), tall)
     for row in range(own_rows):
         for sub in range(SPLIT):
-            start = row * depth + sub * tall
-            out_ref[sub, row, place] = result[start : start + tall]
-
-
-def own_kernel(heads, cols, own_rows, block_ref, w_proj_ref, w_out_ref, made_ref, out_ref, bias_ref):
-    project(heads, cols, own_rows, block_ref, w_proj_ref, w_out_ref, made_ref)
+            out_ref[sub, row, place] = gated[row][sub * tall : (sub + 1) * tall]
+
+
+def own_kernel(heads, cols, own_rows, block_ref, w_proj_ref, made_ref, out_ref, bias_ref):
+    project(heads, cols, own_rows, block_ref, w_proj_ref, made_ref)
     core = lax.axis_index("row") % CORES
     attend(heads, cols, core, block_ref, made_ref, out_ref, bias_ref)
 
@@ -172,6 +168,10 @@
     del half_ref
     core = 1 - lax.axis_index("row") % CORES
     attend(heads, cols, core, other_ref, made_ref, out_ref, bias_ref)
+
+
+def update_kernel(gated_ref, w_out_ref, out_ref):
+    out_ref[...] = jnp.dot(gated_ref[...], w_out_ref[...], preferred_element_type=F32).astype(BF16)
 
 
 def on_device(pair, w_proj, w_bias, w_out, token_mask, *, row_size, col_size):
@@ -217,18 +217,18 @@
     swap = [(r, r ^ 1) for r in range(row_size)]
     other = lax.ppermute(block[:, part:], "row", swap)
 
-    made_shape = jax.ShapeDtypeStruct((own_rows + 1, keys_count + queries, 2 * width), BF16)
+    made_shape = jax.ShapeDtypeStruct((own_rows, keys_count + queries, 2 * width), BF16)
     answer_shape = jax.ShapeDtypeStruct((SPLIT, own_rows, cols, width), BF16)
     scratch = [pltpu.VMEM((heads, depth, keys_count), F32)]
     params = pltpu.CompilerParams(vmem_limit_bytes=12 << 20)
     made, answer = pl.pallas_call(
         functools.partial(own_kernel, heads, cols, own_rows),
         out_shape=(made_shape, answer_shape),
-        in_specs=[VMEM, VMEM, VMEM],
+        in_specs=[VMEM, VMEM],
         out_specs=(VMEM, VMEM),
         scratch_shapes=scratch,
         compiler_params=params,
-    )(block, w_proj, w_out)
+    )(block, w_proj)
     answer = pl.pallas_call(
         functools.partial(other_kernel, heads, cols),
         out_shape=answer_shape,
@@ -241,7 +241,15 @@
 
     near = [[joined(group, sub) for sub in range(SPLIT)] for group in range(SPLIT)]
     answer = answer.reshape(rows, cols, width)
-    return lax.all_to_all(answer, "col", 0, 0, axis_index_groups=near, tiled=True)
+    back = lax.all_to_all(answer, "col", 0, 0, axis_index_groups=near, tiled=True)
+    update = pl.pallas_call(
+        update_kernel,
+        out_shape=jax.ShapeDtypeStruct((rows * cols, width), BF16),
+        in_specs=[VMEM, VMEM],
+        out_specs=VMEM,
+        compiler_params=pltpu.CompilerParams(vmem_limit_bytes=4 << 20),
+    )(back.reshape(rows * cols, width), w_out)
+    return update.reshape(rows, cols, width)
 
 
 def solution(mesh):

time: 65.9 us -> 65.8 us (level)
    pallas_call x0 -> x1, Pallas kernels: none -> 0.83 us  [on_device(): pl.pallas_call(update_kernel, out_shape=jax.ShapeDtypeStruct((rows * cols...]
where the time goes in v9:
time: 65.8 us; the launch traced here: 65.5 us
  blocking collectives  54.3 us (83%)
  starting transfers between devices  6.32 us (10%)
  Pallas kernels  4.71 us (7%)
    all_to_all x1, blocking collectives, on_device(): block = lax.all_to_all(send, 'col', 0, 0, tiled=True)  24.7 us
    all_to_all x1, blocking collectives, on_device(): lax.all_to_all(spread, 'row', 0, 0, axis_index_groups=same_core, tiled=True)  22.2 us
    all_to_all x1, blocking collectives, on_device(): lax.all_to_all(answer, 'col', 0, 0, axis_index_groups=near, tiled=True)  7.38 us
    ppermute x1, starting transfers between devices, on_device(): other = lax.ppermute(block[:, part:], 'row', swap)  6.32 us
    pallas_call x1, Pallas kernels, on_device(): pl.pallas_call(functools.partial(norm_kernel, rows, cols), out_shape=(jax...  1.39 us
    pallas_call x1, Pallas kernels, on_device(): pl.pallas_call(functools.partial(own_kernel, heads, cols, own_rows), out_...  1.33 us
  transfers between devices with their start and end apart: 1, of which 0 were waited for; matrix products, arithmetic and copies ran while one was open for 0% of the time, Pallas kernels for 2%

profile of v9, /device:TPU:1, one launch (start us, length us, event | category | flops | bytes accessed | tf_op | source)
XLA Modules:
  0.0 65.5 jit_solution(7739565881853491211)
XLA Ops:
  0.0 1.4 %shard_map.55 = (bf16[16,192,128]{2,1,0:T(8,128)(2,1)S(1)}, bf16[16,16,128]{2,1,0:T(8,128)(2,1)S(1)}) custom-call(bf16[512,128]{1,0:T(8,128)(2,1)} %bitcast.12, bf16[4,128]{1,0:T(4,128)(2,1)} %bitcast.13, s32[1,32]{1,0:T(1,128)} %bitcast.14), custom_call_target="tpu_custom_call" | custom-call | tf_op jit(solution)/shard_map/pallas_call | solution.py:189
  1.4 22.2 %all_to_all.15 = bf16[16,16,128]{2,1,0:T(8,128)(2,1)S(1)} all-to-all(bf16[16,16,128]{2,1,0:T(8,128)(2,1)S(1)} %get-tuple-element.10), channel_id=1, replica_groups={{0,32,256,288,64,96,320,352,128,160,384,416,192,224,448,480},{16,48,272..., dimensions={0} | all-to-all | bytes 131072 | tf_op jit(solution)/shard_map/all_to_all | solution.py:210
  23.6 0.0 copy-start
  23.7 24.7 %all_to_all.16.block_ref = bf16[16,192,128]{2,1,0:T(8,128)(2,1)S(1)} all-to-all(bf16[16,192,128]{2,1,0:T(8,128)(2,1)S(1)} %constant_dynamic-update-slice_fusion), channel_id=1, replica_groups=mesh['row'=32,'col'=16] {'col'}, dimensions={0} | all-to-all | bytes 1572864 | tf_op jit(solution)/shard_map/all_to_all | solution.py:215
  48.4 0.0 copy-start.1
  48.4 6.3 %collective-permute-start = (bf16[16,64,128]{2,1,0:T(8,128)(2,1)S(1)}, bf16[16,64,128]{2,1,0:T(8,128)(2,1)S(1)}, u32[]{:S(2)}, u32[]{:S(2)}) collective-permute-start(bf16[16,64,128]{2,1,0:T(8,128)(2,1)S(1)} %slice.4), channel_id=1, source_target_pairs={{0,16},{16,0},{32,48},{48,32},{64,80},{80,64},{96,112},{112,96},{1... | collective-permute-start | bytes 786440 | tf_op jit(solution)/shard_map/ppermute | solution.py:218
  54.8 0.0 copy-done
  54.8 1.3 %shard_map.56 = (bf16[4,640,256]{2,1,0:T(8,128)(2,1)S(1)}, bf16[4,4,32,128]{3,2,1,0:T(8,128)(2,1)S(1)}) custom-call(bf16[16,192,128]{2,1,0:T(8,128)(2,1)S(1)} %all_to_all.16.block_ref, bf16[128,512]{1,0:T(8,128)(2,1)S(1)} %copy-done), custom_call_target="tpu_custom_call" | custom-call | tf_op jit(solution)/shard_map/pallas_call | solution.py:224
  56.1 0.0 collective-permute-done.other_ref
  56.1 1.2 %shard_map.57 = bf16[4,4,32,128]{3,2,1,0:T(8,128)(2,1)S(1)} custom-call(bf16[16,64,128]{2,1,0:T(8,128)(2,1)S(1)} %collective-permute-done.other_ref, bf16[4,640,256]{2,1,0:T(8,128)(2,1)S(1)} %get-tuple-element.11.made_ref, bf16[4,4,32,128]{3,2,1,0:T(8,128)(2,1)S(1)} %get-tuple-element.12.half_ref), custom_call_target="tpu_custom_call", output_to_operand_aliasing={{}: (2, {})} | custom-call | tf_op jit(solution)/shard_map/pallas_call | solution.py:232
  57.3 7.4 %all_to_all.17 = bf16[16,32,128]{2,1,0:T(8,128)(2,1)S(1)} all-to-all(bf16[16,32,128]{2,1,0:T(8,128)(2,1)S(1)} %bitcast.8), channel_id=1, replica_groups={{0,1,8,9},{2,3,10,11},{4,5,12,13},{6,7,14,15},{16,17,24,25},{18,19,26,2..., dimensions={0} | all-to-all | bytes 262144 | tf_op jit(solution)/shard_map/all_to_all | solution.py:244
  64.7 0.0 copy-done.1
  64.7 0.8 %shard_map.58 = bf16[512,128]{1,0:T(8,128)(2,1)} custom-call(bf16[512,128]{1,0:T(8,128)(2,1)S(1)} %bitcast.9, bf16[128,128]{1,0:T(8,128)(2,1)S(1)} %copy-done.1), custom_call_target="tpu_custom_call" | custom-call | tf_op jit(solution)/shard_map/pallas_call | solution.py:245
  (3 shorter events, 0.1 us)
Async XLA Ops:
  23.6 31.2 %copy-start = (bf16[128,512]{1,0:T(8,128)(2,1)S(1)}, bf16[128,512]{1,0:T(8,128)(2,1)}, u32[]{:S(2)}) copy-start(bf16[128,512]{1,0:T(8,128)(2,1)} %w_proj_ref.1) | copy-start | bytes 393220
  48.4 16.2 %copy-start.1 = (bf16[128,128]{1,0:T(8,128)(2,1)S(1)}, bf16[128,128]{1,0:T(8,128)(2,1)}, u32[]{:S(2)}) copy-start(bf16[128,128]{1,0:T(8,128)(2,1)} %w_out_ref.1) | copy-start | bytes 98308
  48.4 7.7 %collective-permute-start = (bf16[16,64,128]{2,1,0:T(8,128)(2,1)S(1)}, bf16[16,64,128]{2,1,0:T(8,128)(2,1)S(1)}, u32[]{:S(2)}, u32[]{:S(2)}) collective-permute-start(bf16[16,64,128]{2,1,0:T(8,128)(2,1)S(1)} %slice.4), channel_id=1, source_target_pairs={{0,16},{16,0},{32,48},{48,32},{64,80},{80,64},{96,112},{112,96},{1... | collective-permute-start | bytes 786440 | tf_op jit(solution)/shard_map/ppermute | solution.py:218

commit v10 on v9

--- a/solution.py
+++ b/solution.py
@@ -170,8 +170,18 @@
     attend(heads, cols, core, other_ref, made_ref, out_ref, bias_ref)
 
 
-def update_kernel(gated_ref, w_out_ref, out_ref):
-    out_ref[...] = jnp.dot(gated_ref[...], w_out_ref[...], preferred_element_type=F32).astype(BF16)
+def update_kernel(gated_ref, w_out_ref, out_hbm, made_ref, sent):
+    size = gated_ref.shape[0] // 2
+    copies = []
+    for half in range(2):
+        chosen = slice(half * size, (half + 1) * size)
+        result = jnp.dot(gated_ref[chosen], w_out_ref[...], preferred_element_type=F32)
+        made_ref[chosen] = result.astype(BF16)
+        rows = pl.ds(half * size, size)
+        copies.append(pltpu.make_async_copy(made_ref.at[rows], out_hbm.at[rows], sent.at[half]))
+        copies[-1].start()
+    for copy in copies:
+        copy.wait()
 
 
 def on_device(pair, w_proj, w_bias, w_out, token_mask, *, row_size, col_size):
@@ -246,7 +256,8 @@
         update_kernel,
         out_shape=jax.ShapeDtypeStruct((rows * cols, width), BF16),
         in_specs=[VMEM, VMEM],
-        out_specs=VMEM,
+        out_specs=HBM,
+        scratch_shapes=[pltpu.VMEM((rows * cols, width), BF16), pltpu.SemaphoreType.DMA((2,))],
         compiler_params=pltpu.CompilerParams(vmem_limit_bytes=4 << 20),
     )(back.reshape(rows * cols, width), w_out)
     return update.reshape(rows, cols, width)

time: 65.8 us -> 65.8 us (level)
  no operation moved by 1% of the time
where the time goes in v10:
time: 65.8 us; the launch traced here: 65.5 us
  blocking collectives  54.3 us (83%)
  starting transfers between devices  6.32 us (10%)
  Pallas kernels  4.72 us (7%)
    all_to_all x1, blocking collectives, on_device(): block = lax.all_to_all(send, 'col', 0, 0, tiled=True)  24.7 us
    all_to_all x1, blocking collectives, on_device(): lax.all_to_all(spread, 'row', 0, 0, axis_index_groups=same_core, tiled=True)  22.2 us
    all_to_all x1, blocking collectives, on_device(): lax.all_to_all(answer, 'col', 0, 0, axis_index_groups=near, tiled=True)  7.38 us
    ppermute x1, starting transfers between devices, on_device(): other = lax.ppermute(block[:, part:], 'row', swap)  6.32 us
    pallas_call x1, Pallas kernels, on_device(): pl.pallas_call(functools.partial(norm_kernel, rows, cols), out_shape=(jax...  1.39 us
    pallas_call x1, Pallas kernels, on_device(): pl.pallas_call(functools.partial(own_kernel, heads, cols, own_rows), out_...  1.33 us
  transfers between devices with their start and end apart: 1, of which 0 were waited for; matrix products, arithmetic and copies ran while one was open for 0% of the time, Pallas kernels for 2%

profile of v10, /device:TPU:1, one launch (start us, length us, event | category | flops | bytes accessed | tf_op | source)
XLA Modules:
  0.0 65.5 jit_solution(13558655889828805972)
XLA Ops:
  0.0 1.4 %shard_map.55 = (bf16[16,192,128]{2,1,0:T(8,128)(2,1)S(1)}, bf16[16,16,128]{2,1,0:T(8,128)(2,1)S(1)}) custom-call(bf16[512,128]{1,0:T(8,128)(2,1)} %bitcast.12, bf16[4,128]{1,0:T(4,128)(2,1)} %bitcast.13, s32[1,32]{1,0:T(1,128)} %bitcast.14), custom_call_target="tpu_custom_call" | custom-call | tf_op jit(solution)/shard_map/pallas_call | solution.py:199
  1.4 22.2 %all_to_all.15 = bf16[16,16,128]{2,1,0:T(8,128)(2,1)S(1)} all-to-all(bf16[16,16,128]{2,1,0:T(8,128)(2,1)S(1)} %get-tuple-element.10), channel_id=1, replica_groups={{0,32,256,288,64,96,320,352,128,160,384,416,192,224,448,480},{16,48,272..., dimensions={0} | all-to-all | bytes 131072 | tf_op jit(solution)/shard_map/all_to_all | solution.py:220
  23.6 0.0 copy-start
  23.7 24.7 %all_to_all.16.block_ref = bf16[16,192,128]{2,1,0:T(8,128)(2,1)S(1)} all-to-all(bf16[16,192,128]{2,1,0:T(8,128)(2,1)S(1)} %constant_dynamic-update-slice_fusion), channel_id=1, replica_groups=mesh['row'=32,'col'=16] {'col'}, dimensions={0} | all-to-all | bytes 1572864 | tf_op jit(solution)/shard_map/all_to_all | solution.py:225
  48.4 0.0 copy-start.1
  48.4 6.3 %collective-permute-start = (bf16[16,64,128]{2,1,0:T(8,128)(2,1)S(1)}, bf16[16,64,128]{2,1,0:T(8,128)(2,1)S(1)}, u32[]{:S(2)}, u32[]{:S(2)}) collective-permute-start(bf16[16,64,128]{2,1,0:T(8,128)(2,1)S(1)} %slice.4), channel_id=1, source_target_pairs={{0,16},{16,0},{32,48},{48,32},{64,80},{80,64},{96,112},{112,96},{1... | collective-permute-start | bytes 786440 | tf_op jit(solution)/shard_map/ppermute | solution.py:228
  54.8 0.0 copy-done
  54.8 1.3 %shard_map.56 = (bf16[4,640,256]{2,1,0:T(8,128)(2,1)S(1)}, bf16[4,4,32,128]{3,2,1,0:T(8,128)(2,1)S(1)}) custom-call(bf16[16,192,128]{2,1,0:T(8,128)(2,1)S(1)} %all_to_all.16.block_ref, bf16[128,512]{1,0:T(8,128)(2,1)S(1)} %copy-done), custom_call_target="tpu_custom_call" | custom-call | tf_op jit(solution)/shard_map/pallas_call | solution.py:234
  56.1 0.0 collective-permute-done.other_ref
  56.1 1.2 %shard_map.57 = bf16[4,4,32,128]{3,2,1,0:T(8,128)(2,1)S(1)} custom-call(bf16[16,64,128]{2,1,0:T(8,128)(2,1)S(1)} %collective-permute-done.other_ref, bf16[4,640,256]{2,1,0:T(8,128)(2,1)S(1)} %get-tuple-element.11.made_ref, bf16[4,4,32,128]{3,2,1,0:T(8,128)(2,1)S(1)} %get-tuple-element.12.half_ref), custom_call_target="tpu_custom_call", output_to_operand_aliasing={{}: (2, {})} | custom-call | tf_op jit(solution)/shard_map/pallas_call | solution.py:242
  57.3 7.4 %all_to_all.17 = bf16[16,32,128]{2,1,0:T(8,128)(2,1)S(1)} all-to-all(bf16[16,32,128]{2,1,0:T(8,128)(2,1)S(1)} %bitcast.8), channel_id=1, replica_groups={{0,1,8,9},{2,3,10,11},{4,5,12,13},{6,7,14,15},{16,17,24,25},{18,19,26,2..., dimensions={0} | all-to-all | bytes 262144 | tf_op jit(solution)/shard_map/all_to_all | solution.py:254
  64.7 0.0 copy-done.1
  64.7 0.8 %shard_map.58 = bf16[512,128]{1,0:T(8,128)(2,1)} custom-call(bf16[512,128]{1,0:T(8,128)(2,1)S(1)} %bitcast.9, bf16[128,128]{1,0:T(8,128)(2,1)S(1)} %copy-done.1), custom_call_target="tpu_custom_call" | custom-call | tf_op jit(solution)/shard_map/pallas_call | solution.py:255
  (3 shorter events, 0.1 us)
Async XLA Ops:
  23.6 31.2 %copy-start = (bf16[128,512]{1,0:T(8,128)(2,1)S(1)}, bf16[128,512]{1,0:T(8,128)(2,1)}, u32[]{:S(2)}) copy-start(bf16[128,512]{1,0:T(8,128)(2,1)} %w_proj_ref.1) | copy-start | bytes 393220
  48.4 16.2 %copy-start.1 = (bf16[128,128]{1,0:T(8,128)(2,1)S(1)}, bf16[128,128]{1,0:T(8,128)(2,1)}, u32[]{:S(2)}) copy-start(bf16[128,128]{1,0:T(8,128)(2,1)} %w_out_ref.1) | copy-start | bytes 98308
  48.4 7.7 %collective-permute-start = (bf16[16,64,128]{2,1,0:T(8,128)(2,1)S(1)}, bf16[16,64,128]{2,1,0:T(8,128)(2,1)S(1)}, u32[]{:S(2)}, u32[]{:S(2)}) collective-permute-start(bf16[16,64,128]{2,1,0:T(8,128)(2,1)S(1)} %slice.4), channel_id=1, source_target_pairs={{0,16},{16,0},{32,48},{48,32},{64,80},{80,64},{96,112},{112,96},{1... | collective-permute-start | bytes 786440 | tf_op jit(solution)/shard_map/ppermute | solution.py:228
